TPU v7x, 512 devices: a whole 4x8x8 slice. The times are simulated.
512 devices in a mesh: rows: 128 (over y, z, core), chan: 4 (over x).
Axes of the slice: x: 4, y: 8, z: 8, core: 2. Of those that a mesh axis runs over, the one named last changes fastest.
Arguments:
- field: bfloat16 [128, 1024, 1024], P('chan', 'rows'), may hold values from -6 to 6
- cotangent: bfloat16 [128, 1024, 1024], P('chan', 'rows'), may hold values from -6 to 6
- local_kernel: bfloat16 [9, 128, 128], P(None, 'chan'), may hold values from -0.1875 to 0.1875
- spectral_weight: bfloat16 [128, 128, 128, 128], P('rows', None, 'chan'), may hold values from -0.5 to 0.5
- tile_ids: int32 [1024, 16, 6], P('rows'), may hold values from 0 to 8, as said below
- tile_counts: int32 [1024, 16], P('rows'), may hold values from 2 to 6
Outputs:
- grad_field: bfloat16 [128, 1024, 1024], P('chan', 'rows')
- grad_spectral: bfloat16 [128, 128, 128, 128], P('rows', None, 'chan')
- grad_kernel: float32 [9, 128, 128], P(None, 'chan')
Inputs may be any that keep to these rules, and one draw needn't show every extreme that they name: `tile_ids`: entry t names the neighbour offset of t // 3 - 1 rows and t % 3 - 1 columns; the 6 entries of one block's list differ from one another, while lists of different blocks, in the same grid row too, may name the same offsets. Only the first tile_counts entries of a block's list are in use.
All inputs are finite; a program needn't handle non-finite values.
Results may differ from a plain program's by a relative error of at most 0.02.
Values may be sent and summed in bfloat16 or wider, within the bound.
No kernel may reach another device: no remote copies, remote signals or barrier semaphores. Data moves between devices by JAX's collectives and lax.ppermute only.
A program may use at most 128 MiB of HBM per device.

v0:
```python
import functools
import math

import jax
import jax.numpy as jnp
import numpy as np
from jax import lax
from jax.experimental import pallas as pl
from jax.experimental.pallas import tpu as pltpu
from jax.sharding import PartitionSpec as P

MODES = 64
NY = 1024
OFFSETS = 9
BLOCK = 64
F32 = jnp.float32
BF16 = jnp.bfloat16


def basis_table(length, count):
    cells = np.arange(count, dtype=np.int64)
    waves = np.arange(MODES, dtype=np.int64)
    factor = 2.0 * math.pi / length
    cosines = np.cos((cells[:, None] * waves[None, :] % length) * factor)
    sines = np.sin((cells[:, None] * (waves[None, :] + 1) % length) * factor)
    return (2.0 / length) ** 0.5 * np.concatenate([cosines, sines], axis=1)


def two_parts(table):
    high = table.astype(jnp.bfloat16)
    low = (table - high.astype(np.float64)).astype(jnp.bfloat16)
    return high, low


def column_table():
    return np.concatenate(two_parts(np.ascontiguousarray(basis_table(NY, NY).T)), axis=0)


def row_table(devices, rows):
    table = basis_table(devices * rows, devices * rows).reshape(devices, rows * 2 * MODES)
    return np.concatenate(two_parts(table), axis=1)


def dot(left, right, left_dim=1, right_dim=0):
    return lax.dot_general(
        left, right, (((left_dim,), (right_dim,)), ((), ())), preferred_element_type=F32
    )


def call(body, outs, *args, scratch=(), flops=10**8):
    single = isinstance(outs, tuple)
    outs = [outs] if single else outs
    shapes = [jax.ShapeDtypeStruct(*o) for o in outs]
    size = sum(math.prod(a.shape) * a.dtype.itemsize for a in list(args) + shapes)
    vmem = pl.BlockSpec(memory_space=pltpu.VMEM)
    result = pl.pallas_call(
        body,
        out_shape=shapes,
        in_specs=[vmem] * len(args),
        out_specs=[vmem] * len(shapes),
        scratch_shapes=list(scratch),
        compiler_params=pltpu.CompilerParams(vmem_limit_bytes=48 * 2**20),
        cost_estimate=pl.CostEstimate(flops=flops, bytes_accessed=size, transcendentals=0),
    )(*args)
    return result[0] if single else result


def column_spread(values, table):
    both = dot(table, values, 1, 1)
    half = both.shape[0] // 2
    return both[:half] + both[half:]


def spread_body(field_ref, table_ref, out_ref):
    out_ref[...] = column_spread(field_ref[...], table_ref[...]).astype(BF16)


def row_modes(moved, table, rows, natural):
    wide = dot(moved, table, 0, 0)
    span = wide.shape[1] // 2
    wide = wide[:, :span] + wide[:, span:]
    waves = span // rows
    count = wide.shape[0] // rows
    if natural:
        cube = wide.reshape(count, rows, span)
        place = lax.broadcasted_iota(jnp.int32, (count, rows, waves), 1)
        total = jnp.zeros((count, rows, waves), F32)
        for x in range(rows):
            total = jnp.where(place == x, cube[:, :, x * waves : (x + 1) * waves], total)
        return jnp.sum(total, axis=1)
    total = jnp.zeros((count, waves), F32)
    for x in range(rows):
        total = total + wide[x * count : (x + 1) * count, x * waves : (x + 1) * waves]
    return total


def modes_body(moved_ref, table_ref, out_ref, *, rows, natural):
    out_ref[...] = row_modes(moved_ref[...], table_ref[...], rows, natural).astype(BF16)


def row_values(coeffs, table, rows, natural):
    count, waves = coeffs.shape
    blocks = []
    if natural:
        spread = jnp.broadcast_to(coeffs[:, None, :], (count, rows, waves))
        place = lax.broadcasted_iota(jnp.int32, (count, rows, waves), 1)
        for x in range(rows):
            blocks.append(
                jnp.where(place == x, spread, 0.0).reshape(count * rows, waves).astype(BF16)
            )
    else:
        low = coeffs.astype(BF16)
        none = jnp.zeros((count, waves), BF16)
        for x in range(rows):
            blocks.append(jnp.concatenate([low if k == x else none for k in range(rows)], axis=0))
    placed = jnp.concatenate(blocks, axis=1)
    span = rows * waves
    return dot(table[:, :span], placed, 1, 1) + dot(table[:, span:], placed, 1, 1)


def mix_body(weight_ref, modes_ref, table_ref, out_ref, *, rows):
    waves = modes_ref.shape[1]
    own = weight_ref.shape[0] // waves
    modes = modes_ref[...]
    lane = lax.broadcasted_iota(jnp.int32, (own, waves), 1)
    step = 8
    total = jnp.zeros((own, waves), F32)
    for first in range(0, waves, step):
        part = dot(weight_ref[first * own : (first + step) * own], modes)
        for k in range(step):
            total = jnp.where(lane == first + k, part[k * own : (k + 1) * own], total)
    out_ref[...] = row_values(total, table_ref[...], rows, False).astype(BF16)


def local_body(kernel_ref, field_ref, low_ref, high_ref, mask_ref, out_ref, acc_ref, *, own):
    rows = field_ref.shape[1]
    channels = kernel_ref.shape[1]
    for j in range(-1, rows + 1):
        ref = low_ref if j < 0 else high_ref if j == rows else field_ref.at[:, j]
        source = ref[...].reshape(channels, NY)
        first = 3 * max(0, j - rows + 2)
        last = 3 * min(3, j + 2)
        product = dot(kernel_ref[first * own : last * own], source)
        for t in range(first, last):
            x = j - (t // 3 - 1)
            term = product[(t - first) * own : (t - first + 1) * own] * mask_ref[
                x * OFFSETS + t : x * OFFSETS + t + 1
            ]
            slot = (x * 3 + t % 3) * own
            if t // 3 == 2:
                acc_ref[slot : slot + own] = acc_ref[slot : slot + own] + term
            elif t // 3 == 1:
                acc_ref[slot : slot + own] = acc_ref[slot : slot + own] + term
            else:
                acc_ref[slot : slot + own] = term
    for x in range(rows):
        slot = x * 3 * own
        out_ref[x * own : (x + 1) * own] = (
            pltpu.roll(acc_ref[slot : slot + own], 1, 1)
            + acc_ref[slot + own : slot + 2 * own]
            + pltpu.roll(acc_ref[slot + 2 * own : slot + 3 * own], NY - 1, 1)
        )


def slope_of(pre):
    return (
        0.5 * (1.0 + lax.erf(pre * 0.5**0.5))
        + pre * jnp.exp(-0.5 * pre * pre) * (0.5 / math.pi) ** 0.5
    )


def grad_body(
    local_ref,
    back_ref,
    cot_ref,
    table_ref,
    field_ref,
    low_ref,
    high_ref,
    mask_ref,
    pre_ref,
    spread_ref,
    kernel_ref,
    *,
    own,
):
    rows = field_ref.shape[1]
    channels = kernel_ref.shape[1]
    back = back_ref[...]
    z = local_ref[...] + dot(jnp.concatenate([back, back], axis=0), table_ref[...], 0, 0)
    grad = cot_ref[...].astype(F32) * slope_of(z)
    grad_low = grad.astype(BF16)
    pre_ref[...] = grad_low
    spread_ref[...] = column_spread(grad_low, table_ref[...]).astype(BF16)
    grad = grad_low.astype(F32)
    shifted = [pltpu.roll(grad, NY - 1, 1), grad, pltpu.roll(grad, 1, 1)]
    total = [jnp.zeros((3 * own, channels), F32) for _ in range(3)]
    for j in range(-1, rows + 1):
        ref = low_ref if j < 0 else high_ref if j == rows else field_ref.at[:, j]
        source = ref[...].reshape(channels, NY)
        for group in range(3):
            x = j - (group - 1)
            if x < 0 or x >= rows:
                continue
            pieces = []
            for k in range(3):
                t = 3 * group + k
                pieces.append(
                    (
                        shifted[k][x * own : (x + 1) * own]
                        * mask_ref[x * OFFSETS + t : x * OFFSETS + t + 1]
                    ).astype(BF16)
                )
            total[group] = total[group] + dot(jnp.concatenate(pieces, axis=0), source, 1, 1)
    for group in range(3):
        kernel_ref[group * 3 * own : (group + 1) * 3 * own] = total[group]


def back_mix_body(moved_ref, table_ref, weight_ref, modes_ref, out_ref, *, rows):
    grads = row_modes(moved_ref[...], table_ref[...], rows, False).astype(BF16)
    modes_ref[...] = grads
    own, waves = grads.shape
    turned = grads.astype(F32).T
    repeat = waves // own
    wide = jnp.concatenate([turned] * repeat, axis=1)
    lane = lax.broadcasted_iota(jnp.int32, (waves, waves), 1) // own
    row = lax.broadcasted_iota(jnp.int32, (waves, waves), 0)
    total = jnp.zeros((waves, weight_ref.shape[1]), F32)
    step = 2
    for first in range(0, own, step):
        placed = [
            jnp.where(row == repeat * (first + k) + lane, wide, 0.0).astype(BF16)
            for k in range(step)
        ]
        total = total + dot(
            jnp.concatenate(placed, axis=1),
            weight_ref[first * waves : (first + step) * waves],
        )
    out_ref[...] = total.T.astype(BF16)


def back_rows_body(parts_ref, table_ref, out_ref, *, rows):
    parts = parts_ref[...].astype(F32)
    total = parts[0]
    for k in range(1, parts.shape[0]):
        total = total + parts[k]
    out_ref[...] = row_values(total, table_ref[...], rows, True).astype(BF16)


def local_back_body(kernel_ref, grad_ref, mask_ref, out_ref, low_ref, high_ref, acc_ref, *, own):
    rows = grad_ref.shape[1]
    channels = kernel_ref.shape[1]
    for x in range(rows):
        product = dot(kernel_ref[...], grad_ref[:, x].reshape(channels, NY))
        for t in range(OFFSETS):
            term = product[t * own : (t + 1) * own] * mask_ref[x * OFFSETS + t : x * OFFSETS + t + 1]
            target = x + t // 3
            slot = (target * 3 + t % 3) * own
            if t // 3 == 2 or x == 0:
                acc_ref[slot : slot + own] = term
            else:
                acc_ref[slot : slot + own] = acc_ref[slot : slot + own] + term
    for target in range(rows + 2):
        slot = target * 3 * own
        value = (
            pltpu.roll(acc_ref[slot : slot + own], NY - 1, 1)
            + acc_ref[slot + own : slot + 2 * own]
            + pltpu.roll(acc_ref[slot + 2 * own : slot + 3 * own], 1, 1)
        )
        if target == 0:
            low_ref[...] = value.astype(BF16)
        elif target == rows + 1:
            high_ref[...] = value.astype(BF16)
        else:
            out_ref[(target - 1) * own : target * own] = value


def final_body(back_ref, table_ref, local_ref, out_ref):
    back = back_ref[...]
    spectral = dot(jnp.concatenate([back, back], axis=0), table_ref[...], 0, 0)
    out_ref[...] = (spectral + local_ref[...]).astype(BF16)


def tile_masks(tile_ids, tile_counts):
    slots = jnp.arange(tile_ids.shape[-1], dtype=jnp.int32)
    used = slots[None, None, :] < tile_counts[:, :, None]
    labels = jnp.arange(OFFSETS, dtype=jnp.int32)
    hits = (tile_ids[:, None, :, :] == labels[None, :, None, None]) & used[:, None]
    return jnp.any(hits, axis=3).astype(BF16)


def spread_tables(blocks):
    cells = np.arange(NY)
    plain = (cells[None, :] // BLOCK == np.arange(blocks)[:, None]).astype(np.float32)
    moved = np.stack([np.roll(plain, k - 1, axis=1) for k in range(3)])
    return plain.astype(jnp.bfloat16), moved.astype(jnp.bfloat16)


def on_device(field, cotangent, local_kernel, spectral_weight, tile_ids, tile_counts):
    own, rows = field.shape[:2]
    devices = lax.axis_size("rows")
    groups = lax.axis_size("chan")
    channels = own * groups
    waves = 2 * MODES
    cells = own * rows
    table_y = jnp.asarray(column_table())
    table_x = jnp.asarray(row_table(devices, rows))
    forward = [(i, (i + 1) % devices) for i in range(devices)]
    backward = [(i, (i - 1) % devices) for i in range(devices)]
    lines = cells // 128

    def exchange(values):
        return lax.all_to_all(values, "rows", split_axis=0, concat_axis=0, tiled=True)

    weight = spectral_weight.reshape(waves * own, channels)
    field_rows = jnp.transpose(field, (1, 0, 2))
    inputs = lax.all_gather(field_rows, "chan")
    spread = call(
        spread_body, ((devices, cells), BF16), field.reshape(cells, NY), table_y
    ).reshape(devices, lines, 128)
    moved = exchange(spread).reshape(devices, cells)

    plain, turned = spread_tables(tile_ids.shape[1])
    small = tile_masks(tile_ids, tile_counts)
    masks = jnp.einsum("xtb,by->xty", small, plain, preferred_element_type=F32)
    masks = masks.reshape(rows * OFFSETS, NY)
    moved_masks = jnp.einsum(
        "xgkb,kby->xgky", small.reshape(rows, 3, 3, -1), turned, preferred_element_type=F32
    ).reshape(rows * OFFSETS, NY)
    pieces = jnp.transpose(local_kernel.reshape(OFFSETS, own, groups, own), (2, 0, 1, 3))
    kernel_lines = OFFSETS * own * own // 128
    cot_rows = jnp.transpose(cotangent, (1, 0, 2)).reshape(cells, NY)

    modes = call(
        functools.partial(modes_body, rows=rows, natural=True), ((own, waves), BF16), moved, table_x
    )
    sent = jnp.concatenate(
        [
            jnp.broadcast_to(modes[None], (groups, own, waves)),
            pieces.reshape(groups, kernel_lines, 128),
        ],
        axis=1,
    )
    got = lax.all_to_all(sent, "chan", split_axis=0, concat_axis=0, tiled=True)
    all_modes = got[:, :own].reshape(channels, waves)
    kernel_back = (
        jnp.transpose(got[:, own:].reshape(groups, OFFSETS, own, own), (1, 3, 0, 2))
    ).reshape(OFFSETS * own, channels)

    rows_part = call(
        functools.partial(mix_body, rows=rows),
        ((devices, cells), BF16),
        weight,
        all_modes,
        table_x,
    ).reshape(devices, lines, 128)
    back = exchange(rows_part).reshape(devices, cells)

    low = lax.ppermute(inputs[:, rows - 1], "rows", forward)
    high = lax.ppermute(inputs[:, 0], "rows", backward)
    local = call(
        functools.partial(local_body, own=own),
        ((cells, NY), F32),
        local_kernel.reshape(OFFSETS * own, channels),
        inputs,
        low,
        high,
        moved_masks,
        scratch=[pltpu.VMEM((rows * 3 * own, NY), F32)],
        flops=10**9,
    )
    grad_pre, grad_spread, kernel_part = call(
        functools.partial(grad_body, own=own),
        [((cells, NY), BF16), ((devices, cells), BF16), ((OFFSETS * own, channels), F32)],
        local,
        back,
        cot_rows,
        table_y,
        inputs,
        low,
        high,
        moved_masks,
        flops=2 * 10**9,
    )
    all_grad = lax.all_gather(grad_pre.reshape(rows, own, NY), "chan")

    def with_kernel(values, share):
        high_part = share.astype(BF16)
        low_part = (share - high_part.astype(F32)).astype(BF16)
        return jnp.concatenate([values.reshape(devices, lines, 128), high_part, low_part], axis=1)

    holders = OFFSETS * own // 3
    share = kernel_part.reshape(holders, 3, channels)
    share = jnp.pad(share, ((0, devices - holders), (0, 0), (0, 0)))
    grad_moved = exchange(with_kernel(grad_spread, share))
    grad_modes, partial_in = call(
        functools.partial(back_mix_body, rows=rows),
        [((own, waves), BF16), ((channels, waves), BF16)],
        grad_moved[:, :lines].reshape(devices, cells),
        table_x,
        weight,
    )
    kernel_sum = jnp.sum(grad_moved[:, lines:].astype(F32), axis=0)
    kernel_sum = (kernel_sum[:3] + kernel_sum[3:]) * (devices * rows * NY) ** (-0.5)
    parts_in = lax.all_to_all(
        partial_in.reshape(groups, own, waves), "chan", split_axis=0, concat_axis=0, tiled=True
    )
    back_part = call(
        functools.partial(back_rows_body, rows=rows), ((devices, cells), BF16), parts_in, table_x
    )
    final = exchange(
        with_kernel(back_part, jnp.broadcast_to(kernel_sum[None], (devices, 3, channels)))
    )
    left = jnp.transpose(grad_modes).astype(F32)
    right = jnp.transpose(all_modes).astype(F32)
    grad_spectral = (left[None, :, :, None] * right[None, :, None, :]).astype(BF16)

    local_back, to_low, to_high = call(
        functools.partial(local_back_body, own=own),
        [((cells, NY), F32), ((own, NY), BF16), ((own, NY), BF16)],
        kernel_back,
        all_grad,
        masks,
        scratch=[pltpu.VMEM(((rows + 2) * 3 * own, NY), F32)],
        flops=10**9,
    )
    from_high = lax.ppermute(to_low, "rows", backward)
    from_low = lax.ppermute(to_high, "rows", forward)
    local_back = jnp.transpose(local_back.reshape(rows, own, NY), (1, 0, 2))
    local_back = local_back.at[:, 0].add(from_low.astype(F32))
    local_back = local_back.at[:, rows - 1].add(from_high.astype(F32))
    grad_field = call(
        final_body,
        ((cells, NY), BF16),
        final[:, :lines].reshape(devices, cells),
        table_y,
        local_back.reshape(cells, NY),
    ).reshape(own, rows, NY)
    summed = final[:holders, lines:].astype(F32)
    grad_kernel = (summed[:, :3] + summed[:, 3:]).reshape(OFFSETS, own, channels)
    return (grad_field, grad_spectral, grad_kernel)


def solution(mesh):
    placed = (
        P("chan", "rows", None),
        P("chan", "rows", None),
        P(None, "chan", None),
        P("rows", None, "chan", None),
        P("rows", None, None),
        P("rows", None),
    )
    return jax.shard_map(
        on_device,
        mesh=mesh,
        in_specs=placed,
        out_specs=(P("chan", "rows", None), P("rows", None, "chan", None), P(None, "chan", None)),
        check_vma=False,
    )
```

profile of v0, /device:TPU:1, one launch (start us, length us, event | category | flops | bytes accessed | tf_op | source)
XLA Modules:
  0.0 176.2 jit_solution(17447310080749213318)
XLA Ops:
  7.2 2.2 %copy.76 = bf16[32,8,1024]{2,0,1:T(8,128)(2,1)} copy(bf16[32,8,1024]{2,1,0:T(8,128)(2,1)} %param.14) | data formatting | bytes 1048576 | tf_op args[0]
  12.5 18.4 %all-to-all-start = ((bf16[128,2,128]{2,1,0:T(2,128)(2,1)}), bf16[128,2,128]{2,1,0:T(2,128)(2,1)S(1)}, u32[]{:S(2)}, u32[]{:S(2)}) async-start(bf16[128,2,128]{2,1,0:T(2,128)(2,1)} %reshape.181), calls=%async_computation | async-start | bytes 131072 | tf_op jit(solution)/shard_map/all_to_all | solution.py:313
  31.4 11.0 %all-to-all-done = bf16[128,2,128]{2,1,0:T(2,128)(2,1)S(1)} async-done(((bf16[128,2,128]{2,1,0:T(2,128)(2,1)}), bf16[128,2,128]{2,1,0:T(2,128)(2,1)S(1)}, u32[]{:S(2)}, u32[]{:S(2)}) %all-to-all-start) | async-done | bytes 65568 | tf_op jit(solution)/shard_map/all_to_all | solution.py:313
  43.6 4.0 %all-to-all-start.1 = ((bf16[4,104,128]{2,1,0:T(8,128)(2,1)}), bf16[4,104,128]{2,1,0:T(8,128)(2,1)S(1)}, u32[]{:S(2)}, u32[]{:S(2)}) async-start(bf16[4,104,128]{2,1,0:T(8,128)(2,1)} %pad_maximum_fusion.2), calls=%async_computation.1 | async-start | bytes 212992 | tf_op jit(solution)/shard_map/all_to_all | solution.py:344
  47.6 4.9 %all-gather.6.cloned.1.call-done = bf16[32,32,1024]{2,1,0:T(8,128)(2,1)} async-done(((bf16[8,32,1024]{2,1,0:T(8,128)(2,1)}), bf16[32,32,1024]{2,1,0:T(8,128)(2,1)}) %all-gather.6.cloned.1.call-update) | async-done | bytes 2097168 | tf_op jit(solution)/shard_map/all_gather | solution.py:317
  52.6 1.9 %slice_bitcast_fusion = (bf16[4,32,1024]{2,1,0:T(8,128)(2,1)}, bf16[4,32,1024]{2,1,0:T(8,128)(2,1)}) fusion(bf16[4,8,32,1024]{3,2,1,0:T(8,128)(2,1)} %bitcast.71), kind=kLoop, calls=%fused_computation.8 | loop fusion | bytes 1048576 | tf_op jit(solution)/shard_map/squeeze | solution.py:360
  54.4 4.5 %collective-permute-start = (bf16[4,32,1024]{2,1,0:T(8,128)(2,1)}, bf16[4,32,1024]{2,1,0:T(8,128)(2,1)S(1)}, u32[]{:S(2)}, u32[]{:S(2)}) collective-permute-start(bf16[4,32,1024]{2,1,0:T(8,128)(2,1)} %get-tuple-element.46), channel_id=1, source_target_pairs={{0,4},{4,8},{8,12},{12,16},{16,20},{20,24},{24,28},{28,32},{32,36}... | collective-permute-start | bytes 786440 | tf_op jit(solution)/shard_map/ppermute | solution.py:359
  58.9 1.9 %collective-permute-start.1 = (bf16[4,32,1024]{2,1,0:T(8,128)(2,1)}, bf16[4,32,1024]{2,1,0:T(8,128)(2,1)S(1)}, u32[]{:S(2)}, u32[]{:S(2)}) collective-permute-start(bf16[4,32,1024]{2,1,0:T(8,128)(2,1)} %get-tuple-element.45), channel_id=1, source_target_pairs={{0,508},{4,0},{8,4},{12,8},{16,12},{20,16},{24,20},{28,24},{32,28}... | collective-permute-start | bytes 786440 | tf_op jit(solution)/shard_map/ppermute | solution.py:360
  63.0 16.0 %all-to-all-start.2 = ((bf16[128,2,128]{2,1,0:T(2,128)(2,1)}), bf16[128,2,128]{2,1,0:T(2,128)(2,1)}, u32[]{:S(2)}, u32[]{:S(2)}) async-start(bf16[128,2,128]{2,1,0:T(2,128)(2,1)} %reshape.186), calls=%async_computation.2 | async-start | bytes 131072 | tf_op jit(solution)/shard_map/all_to_all | solution.py:313
  81.1 9.2 %all-to-all-done.2 = bf16[128,2,128]{2,1,0:T(2,128)(2,1)} async-done(((bf16[128,2,128]{2,1,0:T(2,128)(2,1)}), bf16[128,2,128]{2,1,0:T(2,128)(2,1)}, u32[]{:S(2)}, u32[]{:S(2)}) %all-to-all-start.2) | async-done | bytes 65568 | tf_op jit(solution)/shard_map/all_to_all | solution.py:313
  91.2 1.6 copy-done.2
  94.3 3.5 %shard_map.125 = (bf16[256,1024]{1,0:T(8,128)(2,1)}, bf16[128,256]{1,0:T(8,128)(2,1)S(1)}, f32[288,128]{1,0:T(8,128)S(1)}) custom-call(f32[256,1024]{1,0:T(8,128)S(1)} %shard_map.121.local_ref, bf16[128,256]{1,0:T(8,128)(2,1)S(1)} %bitcast.82, bf16[256,1024]{1,0:T(8,128)(2,1)S(1)} %bitcast.76, bf16[256,1024]{1,0:T(8,128)(2,1)S(1)} %copy-done.5, ...), custom_call_target="tpu_custom_call" | custom-call | flops 2000000000 | bytes 5816320 | tf_op jit(solution)/shard_map/pallas_call | solution.py:56
  100.5 5.8 %all-to-all-start.3 = ((bf16[128,8,128]{2,1,0:T(8,128)(2,1)}), bf16[128,8,128]{2,1,0:T(8,128)(2,1)S(1)}, u32[]{:S(2)}, u32[]{:S(2)}) async-start(bf16[128,8,128]{2,1,0:T(8,128)(2,1)} %pad_maximum_fusion), calls=%async_computation.3 | async-start | bytes 524288 | tf_op jit(solution)/shard_map/all_to_all | solution.py:313
  106.9 13.9 %all-to-all-done.3 = bf16[128,8,128]{2,1,0:T(8,128)(2,1)S(1)} async-done(((bf16[128,8,128]{2,1,0:T(8,128)(2,1)}), bf16[128,8,128]{2,1,0:T(8,128)(2,1)S(1)}, u32[]{:S(2)}, u32[]{:S(2)}) %all-to-all-start.3) | async-done | bytes 262176 | tf_op jit(solution)/shard_map/all_to_all | solution.py:313
  120.8 1.7 shard_map.126
  122.5 3.3 %all-to-all-start.4 = ((bf16[4,32,128]{2,1,0:T(8,128)(2,1)}), bf16[4,32,128]{2,1,0:T(8,128)(2,1)S(1)}, u32[]{:S(2)}, u32[]{:S(2)}) async-start(bf16[4,32,128]{2,1,0:T(8,128)(2,1)} %bitcast.15), calls=%async_computation.4 | async-start | bytes 65536 | tf_op jit(solution)/shard_map/all_to_all | solution.py:405
  125.9 4.1 %all-to-all-done.4.parts_ref = bf16[4,32,128]{2,1,0:T(8,128)(2,1)S(1)} async-done(((bf16[4,32,128]{2,1,0:T(8,128)(2,1)}), bf16[4,32,128]{2,1,0:T(8,128)(2,1)S(1)}, u32[]{:S(2)}, u32[]{:S(2)}) %all-to-all-start.4) | async-done | bytes 32800 | tf_op jit(solution)/shard_map/all_to_all | solution.py:405
  131.6 8.0 %all-to-all-start.5 = ((bf16[128,8,128]{2,1,0:T(8,128)(2,1)}), bf16[128,8,128]{2,1,0:T(8,128)(2,1)S(1)}, u32[]{:S(2)}, u32[]{:S(2)}) async-start(bf16[128,8,128]{2,1,0:T(8,128)(2,1)} %pad_maximum_fusion.1), calls=%async_computation.5 | async-start | bytes 524288 | tf_op jit(solution)/shard_map/all_to_all | solution.py:313
  142.0 12.0 %all-to-all-done.5 = bf16[128,8,128]{2,1,0:T(8,128)(2,1)S(1)} async-done(((bf16[128,8,128]{2,1,0:T(8,128)(2,1)}), bf16[128,8,128]{2,1,0:T(8,128)(2,1)S(1)}, u32[]{:S(2)}, u32[]{:S(2)}) %all-to-all-start.5) | async-done | bytes 262176 | tf_op jit(solution)/shard_map/all_to_all | solution.py:313
  154.1 1.6 copy-done.8
  155.6 1.6 shard_map.128
  157.2 3.9 %collective-permute-start.2 = (bf16[32,1024]{1,0:T(8,128)(2,1)S(1)}, bf16[32,1024]{1,0:T(8,128)(2,1)S(1)}, u32[]{:S(2)}, u32[]{:S(2)}) collective-permute-start(bf16[32,1024]{1,0:T(8,128)(2,1)S(1)} %get-tuple-element.40), channel_id=1, source_target_pairs={{0,4},{4,8},{8,12},{12,16},{16,20},{20,24},{24,28},{28,32},{32,36}... | collective-permute-start | bytes 196616 | tf_op jit(solution)/shard_map/ppermute | solution.py:428
  162.1 1.9 %collective-permute-start.3 = (bf16[32,1024]{1,0:T(8,128)(2,1)S(1)}, bf16[32,1024]{1,0:T(8,128)(2,1)S(1)}, u32[]{:S(2)}, u32[]{:S(2)}) collective-permute-start(bf16[32,1024]{1,0:T(8,128)(2,1)S(1)} %get-tuple-element.41), channel_id=1, source_target_pairs={{0,508},{4,0},{8,4},{12,8},{16,12},{20,16},{24,20},{28,24},{32,28}... | collective-permute-start | bytes 196616 | tf_op jit(solution)/shard_map/ppermute | solution.py:427
  164.0 3.6 %collective-permute-done.3 = bf16[32,1024]{1,0:T(8,128)(2,1)S(1)} collective-permute-done((bf16[32,1024]{1,0:T(8,128)(2,1)S(1)}, bf16[32,1024]{1,0:T(8,128)(2,1)S(1)}, u32[]{:S(2)}, u32[]{:S(2)}) %collective-permute-start.3) | collective-permute-done | bytes 65568 | tf_op jit(solution)/shard_map/ppermute | solution.py:427
  (96 shorter events, 21.0 us)
Async XLA Ops:
  7.2 35.3 %copy-start = (bf16[128,2048]{1,0:T(8,128)(2,1)S(1)}, bf16[128,2048]{1,0:T(8,128)(2,1)}, u32[]{:S(2)}) copy-start(bf16[128,2048]{1,0:T(8,128)(2,1)} %constant.72.clone.table_ref) | copy-start | bytes 1572868
  7.2 23.8 %copy-start.6 = (bf16[9,32,128]{2,1,0:T(8,128)(2,1)S(1)}, bf16[9,32,128]{2,1,0:T(8,128)(2,1)}, u32[]{:S(2)}) copy-start(bf16[9,32,128]{2,1,0:T(8,128)(2,1)} %param.16) | copy-start | bytes 221188
  7.2 24.2 %copy-start.15 = (s32[8,16]{1,0:T(8,128)S(1)}, s32[8,16]{1,0:T(8,128)}, u32[]{:S(2)}) copy-start(s32[8,16]{1,0:T(8,128)} %param.19) | copy-start | bytes 1540
  7.2 45.4 %all-gather.6.cloned.1.call-start = ((), (), s32[]{:S(2)}) async-start(), calls=%async_computation.7 | async-start | bytes 2621440 | tf_op jit(solution)/shard_map/all_gather | solution.py:317
  11.9 49.0 %copy-start.14 = (s32[8,16,6]{1,0,2:T(8,128)S(1)}, s32[8,16,6]{1,0,2:T(8,128)}, u32[]{:S(2)}) copy-start(s32[8,16,6]{1,0,2:T(8,128)} %param.18) | copy-start | bytes 9220
  11.9 49.7 %copy-start.1 = (bf16[1,128,32,128]{3,2,1,0:T(8,128)(2,1)S(1)}, bf16[1,128,32,128]{3,2,1,0:T(8,128)(2,1)}, u32[]{:S(2)}) copy-start(bf16[1,128,32,128]{3,2,1,0:T(8,128)(2,1)} %param.17) | copy-start | bytes 3145732
  12.5 29.9 %all-to-all-start = ((bf16[128,2,128]{2,1,0:T(2,128)(2,1)}), bf16[128,2,128]{2,1,0:T(2,128)(2,1)S(1)}, u32[]{:S(2)}, u32[]{:S(2)}) async-start(bf16[128,2,128]{2,1,0:T(2,128)(2,1)} %reshape.181), calls=%async_computation | async-start | bytes 131072 | tf_op jit(solution)/shard_map/all_to_all | solution.py:313
  42.4 36.7 %copy-start.10 = (bf16[3,16,1024,1]{2,1,3,0:T(8,128)(2,1)S(1)}, bf16[3,16,1024,1]{2,1,3,0:T(8,128)(2,1)}, u32[]{:S(2)}) copy-start(bf16[3,16,1024,1]{2,1,3,0:T(8,128)(2,1)} %constant.82) | copy-start | bytes 294916
  43.6 17.3 %all-to-all-start.1 = ((bf16[4,104,128]{2,1,0:T(8,128)(2,1)}), bf16[4,104,128]{2,1,0:T(8,128)(2,1)S(1)}, u32[]{:S(2)}, u32[]{:S(2)}) async-start(bf16[4,104,128]{2,1,0:T(8,128)(2,1)} %pad_maximum_fusion.2), calls=%async_computation.1 | async-start | bytes 212992 | tf_op jit(solution)/shard_map/all_to_all | solution.py:344
  54.4 36.8 %collective-permute-start = (bf16[4,32,1024]{2,1,0:T(8,128)(2,1)}, bf16[4,32,1024]{2,1,0:T(8,128)(2,1)S(1)}, u32[]{:S(2)}, u32[]{:S(2)}) collective-permute-start(bf16[4,32,1024]{2,1,0:T(8,128)(2,1)} %get-tuple-element.46), channel_id=1, source_target_pairs={{0,4},{4,8},{8,12},{12,16},{16,20},{20,24},{24,28},{28,32},{32,36}... | collective-permute-start | bytes 786440 | tf_op jit(solution)/shard_map/ppermute | solution.py:359
  58.9 32.2 %collective-permute-start.1 = (bf16[4,32,1024]{2,1,0:T(8,128)(2,1)}, bf16[4,32,1024]{2,1,0:T(8,128)(2,1)S(1)}, u32[]{:S(2)}, u32[]{:S(2)}) collective-permute-start(bf16[4,32,1024]{2,1,0:T(8,128)(2,1)} %get-tuple-element.45), channel_id=1, source_target_pairs={{0,508},{4,0},{8,4},{12,8},{16,12},{20,16},{24,20},{28,24},{32,28}... | collective-permute-start | bytes 786440 | tf_op jit(solution)/shard_map/ppermute | solution.py:360
  60.9 18.2 %copy-start.11 = (pred[8,9,16]{2,0,1:T(8,128)(4,1)}, pred[8,9,16]{2,0,1:T(8,128)(4,1)S(1)}, u32[]{:S(2)}) copy-start(pred[8,9,16]{2,0,1:T(8,128)(4,1)S(1)} %fusion.2) | copy-start | bytes 3460
  63.0 27.3 %all-to-all-start.2 = ((bf16[128,2,128]{2,1,0:T(2,128)(2,1)}), bf16[128,2,128]{2,1,0:T(2,128)(2,1)}, u32[]{:S(2)}, u32[]{:S(2)}) async-start(bf16[128,2,128]{2,1,0:T(2,128)(2,1)} %reshape.186), calls=%async_computation.2 | async-start | bytes 131072 | tf_op jit(solution)/shard_map/all_to_all | solution.py:313
  79.1 75.0 %all-gather.4.cloned.1.call-start = ((), (), s32[]{:S(2)}) async-start(), calls=%async_computation.6 | async-start | bytes 2621440 | tf_op jit(solution)/shard_map/all_gather | solution.py:385
  79.7 14.6 %copy-start.5 = (bf16[256,1024]{1,0:T(8,128)(2,1)S(1)}, bf16[256,1024]{1,0:T(8,128)(2,1)}, u32[]{:S(2)}) copy-start(bf16[256,1024]{1,0:T(8,128)(2,1)} %constant.71.clone.table_ref) | copy-start | bytes 1572868
  91.2 1.6 copy-start.2
  98.5 7.9 %copy-start.12 = (pred[8,9,16]{2,0,1:T(8,128)(4,1)S(1)}, pred[8,9,16]{2,0,1:T(8,128)(4,1)}, u32[]{:S(2)}) copy-start(pred[8,9,16]{2,0,1:T(8,128)(4,1)} %copy-done.11) | copy-start | bytes 3460
  98.5 8.1 %copy-start.13 = (bf16[16,1024]{1,0:T(8,128)(2,1)S(1)}, bf16[16,1024]{1,0:T(8,128)(2,1)}, u32[]{:S(2)}) copy-start(bf16[16,1024]{1,0:T(8,128)(2,1)} %constant.73.clone) | copy-start | bytes 98308
  100.5 20.2 %all-to-all-start.3 = ((bf16[128,8,128]{2,1,0:T(8,128)(2,1)}), bf16[128,8,128]{2,1,0:T(8,128)(2,1)S(1)}, u32[]{:S(2)}, u32[]{:S(2)}) async-start(bf16[128,8,128]{2,1,0:T(8,128)(2,1)} %pad_maximum_fusion), calls=%async_computation.3 | async-start | bytes 524288 | tf_op jit(solution)/shard_map/all_to_all | solution.py:313
  120.8 18.9 %slice-start = ((bf16[4,104,128]{2,1,0:T(8,128)(2,1)}), bf16[4,72,128]{2,1,0:T(8,128)(2,1)S(1)}, s32[]{:S(2)}) async-start(bf16[4,104,128]{2,1,0:T(8,128)(2,1)} %copy-done.9), calls=%async_computation.8 | async-start | bytes 147456 | tf_op jit(solution)/shard_map/slice | solution.py:347
  122.5 7.5 %all-to-all-start.4 = ((bf16[4,32,128]{2,1,0:T(8,128)(2,1)}), bf16[4,32,128]{2,1,0:T(8,128)(2,1)S(1)}, u32[]{:S(2)}, u32[]{:S(2)}) async-start(bf16[4,32,128]{2,1,0:T(8,128)(2,1)} %bitcast.15), calls=%async_computation.4 | async-start | bytes 65536 | tf_op jit(solution)/shard_map/all_to_all | solution.py:405
  131.6 22.4 %all-to-all-start.5 = ((bf16[128,8,128]{2,1,0:T(8,128)(2,1)}), bf16[128,8,128]{2,1,0:T(8,128)(2,1)S(1)}, u32[]{:S(2)}, u32[]{:S(2)}) async-start(bf16[128,8,128]{2,1,0:T(8,128)(2,1)} %pad_maximum_fusion.1), calls=%async_computation.5 | async-start | bytes 524288 | tf_op jit(solution)/shard_map/all_to_all | solution.py:313
  157.2 6.8 %collective-permute-start.2 = (bf16[32,1024]{1,0:T(8,128)(2,1)S(1)}, bf16[32,1024]{1,0:T(8,128)(2,1)S(1)}, u32[]{:S(2)}, u32[]{:S(2)}) collective-permute-start(bf16[32,1024]{1,0:T(8,128)(2,1)S(1)} %get-tuple-element.40), channel_id=1, source_target_pairs={{0,4},{4,8},{8,12},{12,16},{16,20},{20,24},{24,28},{28,32},{32,36}... | collective-permute-start | bytes 196616 | tf_op jit(solution)/shard_map/ppermute | solution.py:428
  162.1 5.6 %collective-permute-start.3 = (bf16[32,1024]{1,0:T(8,128)(2,1)S(1)}, bf16[32,1024]{1,0:T(8,128)(2,1)S(1)}, u32[]{:S(2)}, u32[]{:S(2)}) collective-permute-start(bf16[32,1024]{1,0:T(8,128)(2,1)S(1)} %get-tuple-element.41), channel_id=1, source_target_pairs={{0,508},{4,0},{8,4},{12,8},{16,12},{20,16},{24,20},{28,24},{32,28}... | collective-permute-start | bytes 196616 | tf_op jit(solution)/shard_map/ppermute | solution.py:427
  (5 other events, 5.0 us)
Sparse Core Ops, SparseCore 0:
  10.7 41.8 all-gather.5
  98.6 27.0 all-gather.3
where the time goes:
time: 178 us; the launch traced here: 176 us
  starting transfers between devices  67.9 us (38%)
  waiting for transfers between devices  58.8 us (33%)
  local copies, waits for them, and re-layouts  18.6 us (10%)
  between operations  14.6 us (8%)
  Pallas kernels  11.5 us (6%)
  other arithmetic  4.44 us (2%)
    all_to_all x4, starting transfers between devices, exchange(): lax.all_to_all(values, 'rows', split_axis=0, concat_axis=0, tiled=True)  48.3 us
    all_to_all x4, waiting for transfers between devices, exchange(): lax.all_to_all(values, 'rows', split_axis=0, concat_axis=0, tiled=True)  46.1 us
    pallas_call x9, Pallas kernels, call(): pl.pallas_call(body, out_shape=shapes, in_specs=[vmem] * len(args), out_s...  11.5 us
    unnamed x38, local copies, waits for them, and re-layouts  9.74 us
    all_gather x1, waiting for transfers between devices, on_device(): inputs = lax.all_gather(field_rows, 'chan')  4.94 us
    ppermute x1, starting transfers between devices, on_device(): low = lax.ppermute(inputs[:, rows - 1], 'rows', forward)  4.51 us
    all_to_all x1, waiting for transfers between devices, on_device(): lax.all_to_all(partial_in.reshape(groups, own, waves), 'chan', split_axis...  4.11 us
    all_to_all x1, starting transfers between devices, on_device(): got = lax.all_to_all(sent, 'chan', split_axis=0, concat_axis=0, tiled=True)  4.02 us
  transfers between devices with their start and end apart: 12, of which 7 were waited for; matrix products, arithmetic and copies ran while one was open for 8% of the time, Pallas kernels for 2%

commit v1 on v0

v1 whole, which is shorter than its diff:
```python
import functools
import math

import jax
import jax.numpy as jnp
import numpy as np
from jax import lax
from jax.experimental import pallas as pl
from jax.experimental.pallas import tpu as pltpu
from jax.sharding import PartitionSpec as P

MODES = 64
NY = 1024
OFFSETS = 9
BLOCK = 64
F32 = jnp.float32
BF16 = jnp.bfloat16


def basis_table(length, count):
    cells = np.arange(count, dtype=np.int64)
    waves = np.arange(MODES, dtype=np.int64)
    factor = 2.0 * math.pi / length
    cosines = np.cos((cells[:, None] * waves[None, :] % length) * factor)
    sines = np.sin((cells[:, None] * (waves[None, :] + 1) % length) * factor)
    return (2.0 / length) ** 0.5 * np.concatenate([cosines, sines], axis=1)


def two_parts(table):
    high = table.astype(jnp.bfloat16)
    low = (table - high.astype(np.float64)).astype(jnp.bfloat16)
    return high, low


def column_table():
    return np.concatenate(two_parts(np.ascontiguousarray(basis_table(NY, NY).T)), axis=0)


def row_table(devices, rows):
    table = basis_table(devices * rows, devices * rows).reshape(devices, rows * 2 * MODES)
    return np.concatenate(two_parts(table), axis=1)


def dot(left, right, left_dim=1, right_dim=0):
    return lax.dot_general(
        left, right, (((left_dim,), (right_dim,)), ((), ())), preferred_element_type=F32
    )


def call(body, outs, *args, scratch=(), flops=10**8, far=(), limit=48):
    single = isinstance(outs, tuple)
    outs = [outs] if single else outs
    shapes = [jax.ShapeDtypeStruct(*o) for o in outs]
    size = sum(
        math.prod(a.shape) * a.dtype.itemsize
        for k, a in enumerate(list(args) + shapes)
        if k not in far
    )
    result = pl.pallas_call(
        body,
        out_shape=shapes,
        in_specs=[
            pl.BlockSpec(memory_space=pltpu.HBM if k in far else pltpu.VMEM)
            for k in range(len(args))
        ],
        out_specs=[pl.BlockSpec(memory_space=pltpu.VMEM)] * len(shapes),
        scratch_shapes=list(scratch),
        compiler_params=pltpu.CompilerParams(vmem_limit_bytes=limit * 2**20),
        cost_estimate=pl.CostEstimate(flops=flops, bytes_accessed=size, transcendentals=0),
    )(*args)
    return result[0] if single else result


def every(ref, first, count, stride):
    return ref.at[pl.ds(first, count, stride=stride)]


def put_wide(wide_ref, values):
    for k in range(wide_ref.shape[0]):
        wide_ref[k] = values[:, k * 128 : (k + 1) * 128]


def get_wide(wide_ref):
    return jnp.concatenate([wide_ref[k] for k in range(wide_ref.shape[0])], axis=1)


def wide_rows(wide_ref, first, count, stride):
    return [
        wide_ref.at[k, pl.ds(first, count, stride=stride)] for k in range(wide_ref.shape[0])
    ]


def write_lines(line_ref, values, lines):
    count = values.shape[0]
    every(line_ref, 0, count, lines)[...] = values[:, :128]
    every(line_ref, 1, count, lines)[...] = values[:, 128:]


def read_lines(line_ref, count, lines):
    return jnp.concatenate(
        [every(line_ref, k, count, lines)[...].astype(BF16) for k in range(2)], axis=1
    )


def column_spread(values, table):
    both = dot(table, values, 1, 1)
    half = both.shape[0] // 2
    return both[:half] + both[half:]


def spread_body(
    field_ref, table_ref, out_ref, rows_ref, held, held_table, wide, line_ref, sems, *, rows
):
    field_copy = pltpu.make_async_copy(field_ref, held, sems.at[0])
    table_copy = pltpu.make_async_copy(table_ref, held_table, sems.at[1])
    field_copy.start()
    table_copy.start()
    field_copy.wait()
    put_wide(wide, held[...].astype(F32))
    own = rows_ref.shape[1]
    for x in range(rows):
        views = wide_rows(wide, x, own, rows)
        rows_ref[x] = jnp.concatenate([view[...] for view in views], axis=1).astype(BF16)
    table_copy.wait()
    write_lines(line_ref, column_spread(held[...], held_table[...]), 2)
    out_ref[...] = line_ref[...].astype(BF16)


def row_modes(moved, table, rows, natural):
    wide = dot(moved, table, 0, 0)
    span = wide.shape[1] // 2
    wide = wide[:, :span] + wide[:, span:]
    waves = span // rows
    count = wide.shape[0] // rows
    if natural:
        cube = wide.reshape(count, rows, span)
        place = lax.broadcasted_iota(jnp.int32, (count, rows, waves), 1)
        total = jnp.zeros((count, rows, waves), F32)
        for x in range(rows):
            total = jnp.where(place == x, cube[:, :, x * waves : (x + 1) * waves], total)
        return jnp.sum(total, axis=1)
    total = jnp.zeros((count, waves), F32)
    for x in range(rows):
        total = total + wide[x * count : (x + 1) * count, x * waves : (x + 1) * waves]
    return total


def modes_body(moved_ref, table_ref, piece_ref, ready_ref, out_ref, line_ref, *, rows):
    line_ref[...] = moved_ref[...].astype(F32)
    modes = row_modes(read_lines(line_ref, table_ref.shape[0], 2), table_ref[...], rows, True)
    own = modes.shape[0]
    for k in range(out_ref.shape[0]):
        out_ref[k, :own] = modes.astype(BF16)
        out_ref[k, own:] = piece_ref[k]


def row_values(coeffs, table, rows, natural):
    count, waves = coeffs.shape
    blocks = []
    if natural:
        spread = jnp.broadcast_to(coeffs[:, None, :], (count, rows, waves))
        place = lax.broadcasted_iota(jnp.int32, (count, rows, waves), 1)
        for x in range(rows):
            blocks.append(
                jnp.where(place == x, spread, 0.0).reshape(count * rows, waves).astype(BF16)
            )
    else:
        low = coeffs.astype(BF16)
        none = jnp.zeros((count, waves), BF16)
        for x in range(rows):
            blocks.append(jnp.concatenate([low if k == x else none for k in range(rows)], axis=0))
    placed = jnp.concatenate(blocks, axis=1)
    span = rows * waves
    return dot(table[:, :span], placed, 1, 1) + dot(table[:, span:], placed, 1, 1)


def mix_body(weight_ref, got_ref, table_ref, plain_ref, turned_ref, out_ref, line_ref, *, rows):
    waves = got_ref.shape[2]
    own = weight_ref.shape[0] // waves
    modes = got_ref[:, :own].reshape(got_ref.shape[0] * own, waves)
    lane = lax.broadcasted_iota(jnp.int32, (own, waves), 1)
    step = 8
    total = jnp.zeros((own, waves), F32)
    for first in range(0, waves, step):
        part = dot(weight_ref[first * own : (first + step) * own], modes)
        for k in range(step):
            total = jnp.where(lane == first + k, part[k * own : (k + 1) * own], total)
    line_ref[...] = jnp.zeros(line_ref.shape, F32)
    write_lines(line_ref, row_values(total, table_ref[...], rows, False), 8)
    out_ref[...] = line_ref[...].astype(BF16)


def edges_body(field_ref, after_ref, low_ref, high_ref, sems):
    rows = field_ref.shape[1]
    copies = [
        pltpu.make_async_copy(field_ref.at[:, rows - 1], low_ref, sems.at[0]),
        pltpu.make_async_copy(field_ref.at[:, 0], high_ref, sems.at[1]),
    ]
    for copy in copies:
        copy.start()
    for copy in copies:
        copy.wait()


def local_body(kernel_ref, field_ref, mask_ref, out_ref, acc_ref, *, own):
    rows = field_ref.shape[1]
    channels = kernel_ref.shape[1]
    for j in range(rows):
        source = field_ref[:, j].reshape(channels, NY)
        first = 3 * max(0, j - rows + 2)
        last = 3 * min(3, j + 2)
        product = dot(kernel_ref[first * own : last * own], source)
        for t in range(first, last):
            x = j - (t // 3 - 1)
            term = product[(t - first) * own : (t - first + 1) * own] * mask_ref[
                x * OFFSETS + t : x * OFFSETS + t + 1
            ]
            slot = (x * 3 + t % 3) * own
            if t // 3 == 0 or j == 0:
                acc_ref[slot : slot + own] = term
            else:
                acc_ref[slot : slot + own] = acc_ref[slot : slot + own] + term
    for x in range(rows):
        slot = x * 3 * own
        out_ref[x * own : (x + 1) * own] = turn_back(
            [acc_ref[slot + k * own : slot + (k + 1) * own] for k in range(3)]
        )


def turn_back(parts):
    return pltpu.roll(parts[0], 1, 1) + parts[1] + pltpu.roll(parts[2], NY - 1, 1)


def slope_of(pre):
    return (
        0.5 * (1.0 + lax.erf(pre * 0.5**0.5))
        + pre * jnp.exp(-0.5 * pre * pre) * (0.5 / math.pi) ** 0.5
    )


def write_shares(line_ref, shares, lines, holders, devices):
    for k, share in enumerate(shares):
        high = share.astype(BF16).astype(F32)
        for line, value in ((2 + k, high), (5 + k, share - high)):
            every(line_ref, line, holders, lines)[...] = value
            if holders < devices:
                every(line_ref, holders * lines + line, devices - holders, lines)[...] = jnp.zeros(
                    (devices - holders, value.shape[1]), F32
                )


def grad_body(
    local_ref,
    back_ref,
    cot_ref,
    table_ref,
    field_ref,
    low_ref,
    high_ref,
    mask_ref,
    kernel_ref,
    pre_ref,
    out_ref,
    z_ref,
    back_lines,
    share_ref,
    line_ref,
    *,
    own,
    devices,
):
    rows = field_ref.shape[1]
    channels = kernel_ref.shape[1]
    back_lines[...] = back_ref[...].astype(F32)
    back = read_lines(back_lines, devices, 8)
    z_ref[...] = local_ref[...] + dot(
        jnp.concatenate([back, back], axis=0), table_ref[...], 0, 0
    )
    for x, first, ref in ((0, 0, low_ref), (rows - 1, 6, high_ref)):
        product = dot(
            kernel_ref[first * own : (first + 3) * own], ref[...].reshape(channels, NY)
        )
        parts = [
            product[k * own : (k + 1) * own]
            * mask_ref[x * OFFSETS + first + k : x * OFFSETS + first + k + 1]
            for k in range(3)
        ]
        z_ref[x * own : (x + 1) * own] = z_ref[x * own : (x + 1) * own] + turn_back(parts)
    grad = cot_ref[...].astype(F32) * slope_of(z_ref[...])
    grad_low = grad.astype(BF16)
    pre_ref[...] = grad_low
    write_lines(line_ref, column_spread(grad_low, table_ref[...]), 8)
    grad = grad_low.astype(F32)
    shifted = [pltpu.roll(grad, NY - 1, 1), grad, pltpu.roll(grad, 1, 1)]
    total = [jnp.zeros((3 * own, channels), F32) for _ in range(3)]
    for j in range(-1, rows + 1):
        ref = low_ref if j < 0 else high_ref if j == rows else field_ref.at[:, j]
        source = ref[...].reshape(channels, NY)
        for group in range(3):
            x = j - (group - 1)
            if x < 0 or x >= rows:
                continue
            pieces = []
            for k in range(3):
                t = 3 * group + k
                pieces.append(
                    (
                        shifted[k][x * own : (x + 1) * own]
                        * mask_ref[x * OFFSETS + t : x * OFFSETS + t + 1]
                    ).astype(BF16)
                )
            total[group] = total[group] + dot(jnp.concatenate(pieces, axis=0), source, 1, 1)
    for group in range(3):
        share_ref[group * 3 * own : (group + 1) * 3 * own] = total[group]
    holders = 3 * own
    write_shares(
        line_ref, [every(share_ref, k, holders, 3)[...] for k in range(3)], 8, holders, devices
    )
    out_ref[...] = line_ref[...].astype(BF16)


def back_mix_body(
    moved_ref, table_ref, weight_ref, modes_ref, out_ref, sum_ref, line_ref, *, rows, scale
):
    devices = table_ref.shape[0]
    line_ref[...] = moved_ref[...].astype(F32)
    grads = row_modes(read_lines(line_ref, devices, 8), table_ref[...], rows, False).astype(BF16)
    modes_ref[...] = grads
    own, waves = grads.shape
    turned = grads.astype(F32).T
    repeat = waves // own
    wide = jnp.concatenate([turned] * repeat, axis=1)
    lane = lax.broadcasted_iota(jnp.int32, (waves, waves), 1) // own
    row = lax.broadcasted_iota(jnp.int32, (waves, waves), 0)
    total = jnp.zeros((waves, weight_ref.shape[1]), F32)
    step = 2
    for first in range(0, own, step):
        placed = [
            jnp.where(row == repeat * (first + k) + lane, wide, 0.0).astype(BF16)
            for k in range(step)
        ]
        total = total + dot(
            jnp.concatenate(placed, axis=1),
            weight_ref[first * waves : (first + step) * waves],
        )
    out_ref[...] = total.T.astype(BF16)
    sums = line_ref[0:8]
    for r in range(1, devices):
        sums = sums + line_ref[r * 8 : (r + 1) * 8]
    sum_ref[...] = sums * scale


def back_rows_body(parts_ref, table_ref, sum_ref, *refs, rows):
    out_ref, line_ref = refs[-2:]
    parts = parts_ref[...].astype(F32)
    total = parts[0]
    for k in range(1, parts.shape[0]):
        total = total + parts[k]
    devices = table_ref.shape[0]
    write_lines(line_ref, row_values(total, table_ref[...], rows, True), 8)
    shares = [
        jnp.broadcast_to(
            sum_ref[2 + k : 3 + k] + sum_ref[5 + k : 6 + k], (devices, sum_ref.shape[1])
        )
        for k in range(3)
    ]
    write_shares(line_ref, shares, 8, devices, devices)
    out_ref[...] = line_ref[...].astype(BF16)


def edge_back_body(kernel_ref, grad_ref, mask_ref, low_ref, high_ref, *, own):
    rows = grad_ref.shape[1]
    channels = kernel_ref.shape[1]
    for x, first, ref in ((0, 0, low_ref), (rows - 1, 6, high_ref)):
        product = dot(
            kernel_ref[first * own : (first + 3) * own], grad_ref[:, x].reshape(channels, NY)
        )
        parts = [
            product[k * own : (k + 1) * own]
            * mask_ref[x * OFFSETS + first + k : x * OFFSETS + first + k + 1]
            for k in (2, 1, 0)
        ]
        ref[...] = turn_back(parts).astype(BF16)


def local_back_body(kernel_ref, grad_ref, mask_ref, out_ref, acc_ref, *, own):
    rows = grad_ref.shape[1]
    channels = kernel_ref.shape[1]
    for x in range(rows):
        first = 3 if x == 0 else 0
        last = 6 if x == rows - 1 else 9
        product = dot(
            kernel_ref[first * own : last * own], grad_ref[:, x].reshape(channels, NY)
        )
        for t in range(first, last):
            term = product[(t - first) * own : (t - first + 1) * own] * mask_ref[
                x * OFFSETS + t : x * OFFSETS + t + 1
            ]
            slot = ((x + t // 3 - 1) * 3 + t % 3) * own
            if t // 3 == 2 or (x == 0 and t // 3 == 1):
                acc_ref[slot : slot + own] = term
            else:
                acc_ref[slot : slot + own] = acc_ref[slot : slot + own] + term
    for target in range(rows):
        slot = target * 3 * own
        value = turn_back(
            [acc_ref[slot + k * own : slot + (k + 1) * own] for k in (2, 1, 0)]
        )
        for k, view in enumerate(wide_rows(out_ref, target, own, rows)):
            view[...] = value[:, k * 128 : (k + 1) * 128]


def final_body(
    moved_ref, table_ref, local_ref, low_ref, high_ref, out_ref, share_ref, line_ref, sum_ref
):
    own = low_ref.shape[0]
    rows = local_ref.shape[1] // own
    devices = table_ref.shape[0] // 2
    holders = share_ref.shape[0] // 3
    line_ref[...] = moved_ref[...].astype(F32)
    back = read_lines(line_ref, devices, 8)
    for x, ref in ((0, low_ref), (rows - 1, high_ref)):
        edge = ref[...].astype(F32)
        for k, view in enumerate(wide_rows(sum_ref, x, own, rows)):
            view[...] = edge[:, k * 128 : (k + 1) * 128]
    for x in range(1, rows - 1):
        for view in wide_rows(sum_ref, x, own, rows):
            view[...] = jnp.zeros((own, 128), F32)
    spectral = dot(jnp.concatenate([back, back], axis=0), table_ref[...], 0, 0)
    out_ref[...] = (spectral + get_wide(local_ref) + get_wide(sum_ref)).astype(BF16)
    for k in range(3):
        every(share_ref, k, holders, 3)[...] = (
            every(line_ref, 2 + k, holders, 8)[...] + every(line_ref, 5 + k, holders, 8)[...]
        )


def tile_masks(tile_ids, tile_counts):
    slots = jnp.arange(tile_ids.shape[-1], dtype=jnp.int32)
    used = slots[None, None, :] < tile_counts[:, :, None]
    labels = jnp.arange(OFFSETS, dtype=jnp.int32)
    hits = (tile_ids[:, None, :, :] == labels[None, :, None, None]) & used[:, None]
    return jnp.any(hits, axis=3).astype(BF16)


def spread_tables(blocks):
    cells = np.arange(NY)
    plain = (cells[None, :] // BLOCK == np.arange(blocks)[:, None]).astype(np.float32)
    moved = np.stack([np.roll(plain, k - 1, axis=1) for k in range(3)])
    return plain.astype(jnp.bfloat16), moved.astype(jnp.bfloat16)


def on_device(field, cotangent, local_kernel, spectral_weight, tile_ids, tile_counts):
    own, rows = field.shape[:2]
    devices = lax.axis_size("rows")
    groups = lax.axis_size("chan")
    channels = own * groups
    waves = 2 * MODES
    cells = own * rows
    table_y = jnp.asarray(column_table())
    table_x = jnp.asarray(row_table(devices, rows))
    forward = [(i, (i + 1) % devices) for i in range(devices)]
    backward = [(i, (i - 1) % devices) for i in range(devices)]
    def exchange(lines):
        cube = lines.reshape(devices, -1, 128)
        moved = lax.all_to_all(cube, "rows", split_axis=0, concat_axis=0, tiled=True)
        return moved.reshape(lines.shape)

    def swap(values):
        return lax.all_to_all(values, "chan", split_axis=0, concat_axis=0, tiled=True)

    weight = spectral_weight.reshape(waves * own, channels)
    two = pltpu.VMEM((2 * devices, 128), F32)
    eight = pltpu.VMEM((8 * devices, 128), F32)
    wide = pltpu.VMEM((NY // 128, cells, 128), F32)
    spread, field_rows = call(
        functools.partial(spread_body, rows=rows),
        [((2 * devices, 128), BF16), ((rows, own, NY), BF16)],
        field.reshape(cells, NY),
        table_y,
        far=(0, 1),
        limit=61,
        scratch=[
            pltpu.VMEM((cells, NY), BF16),
            pltpu.VMEM(table_y.shape, BF16),
            wide,
            two,
            pltpu.SemaphoreType.DMA((2,)),
        ],
    )
    inputs = lax.all_gather(field_rows, "chan")
    moved = exchange(spread)

    pieces = jnp.transpose(local_kernel.reshape(OFFSETS, own, groups, own), (2, 0, 1, 3))
    pieces = pieces.reshape(groups, OFFSETS * own * own // 128, 128)
    kernel_lines = pieces.shape[1]
    pieces = jnp.pad(pieces, ((0, 0), (0, -kernel_lines % 16), (0, 0)))
    cot_rows = jnp.transpose(cotangent, (1, 0, 2)).reshape(cells, NY)
    plain, turned = spread_tables(tile_ids.shape[1])
    small = tile_masks(tile_ids, tile_counts)
    masks = jnp.einsum("xtb,by->xty", small, plain, preferred_element_type=F32)
    masks = masks.reshape(rows * OFFSETS, NY)
    moved_masks = jnp.einsum(
        "xgkb,kby->xgky", small.reshape(rows, 3, 3, -1), turned, preferred_element_type=F32
    ).reshape(rows * OFFSETS, NY)

    sent = call(
        functools.partial(modes_body, rows=rows),
        ((groups, own + pieces.shape[1], waves), BF16),
        moved,
        table_x,
        pieces,
        cot_rows,
        far=(3,),
        scratch=[two],
    )
    got = swap(sent)
    rows_part = call(
        functools.partial(mix_body, rows=rows),
        ((8 * devices, 128), BF16),
        weight,
        got,
        table_x,
        masks,
        moved_masks,
        far=(3, 4),
        scratch=[pltpu.VMEM((8 * devices, 128), F32)],
    )
    back = exchange(rows_part)
    low, high = call(
        edges_body,
        [((groups, own, NY), BF16)] * 2,
        inputs,
        rows_part,
        far=(0, 1),
        scratch=[pltpu.SemaphoreType.DMA((2,))],
    )
    low = lax.ppermute(low, "rows", forward)
    high = lax.ppermute(high, "rows", backward)
    kernel_rows = local_kernel.reshape(OFFSETS * own, channels)
    local = call(
        functools.partial(local_body, own=own),
        ((cells, NY), F32),
        kernel_rows,
        inputs,
        moved_masks,
        scratch=[pltpu.VMEM((rows * 3 * own, NY), F32)],
        flops=10**9,
    )
    grad_pre, grad_spread = call(
        functools.partial(grad_body, own=own, devices=devices),
        [((cells, NY), BF16), ((8 * devices, 128), BF16)],
        local,
        back,
        cot_rows,
        table_y,
        inputs,
        low,
        high,
        moved_masks,
        kernel_rows,
        scratch=[
            pltpu.VMEM((cells, NY), F32),
            pltpu.VMEM((8 * devices, 128), F32),
            pltpu.VMEM((OFFSETS * own, channels), F32),
            eight,
        ],
        flops=2 * 10**9,
    )
    all_grad = lax.all_gather(grad_pre.reshape(rows, own, NY), "chan")
    grad_moved = exchange(grad_spread)
    grad_modes, partial_in, kernel_sum = call(
        functools.partial(back_mix_body, rows=rows, scale=(devices * rows * NY) ** (-0.5)),
        [((own, waves), BF16), ((channels, waves), BF16), ((8, channels), F32)],
        grad_moved,
        table_x,
        weight,
        scratch=[eight],
    )
    parts_in = swap(partial_in.reshape(groups, own, waves))
    all_modes = got[:, :own].reshape(channels, waves)
    kernel_back = (
        jnp.transpose(
            got[:, own : own + kernel_lines].reshape(groups, OFFSETS, own, own), (1, 3, 0, 2)
        )
    ).reshape(OFFSETS * own, channels)
    left = jnp.transpose(grad_modes).astype(F32)
    right = jnp.transpose(all_modes).astype(F32)
    grad_spectral = (left[None, :, :, None] * right[None, :, None, :]).astype(BF16)
    back_part = call(
        functools.partial(back_rows_body, rows=rows),
        ((8 * devices, 128), BF16),
        parts_in,
        table_x,
        kernel_sum,
        all_grad[0, 0, :16, :128],
        grad_spectral,
        kernel_back,
        far=(4, 5),
        scratch=[eight],
    )
    final = exchange(back_part)
    to_low, to_high = call(
        functools.partial(edge_back_body, own=own),
        [((own, NY), BF16), ((own, NY), BF16)],
        kernel_back,
        all_grad,
        masks,
    )
    from_high = lax.ppermute(to_low, "rows", backward)
    from_low = lax.ppermute(to_high, "rows", forward)
    local_back = call(
        functools.partial(local_back_body, own=own),
        ((NY // 128, cells, 128), F32),
        kernel_back,
        all_grad,
        masks,
        scratch=[pltpu.VMEM((rows * 3 * own, NY), F32)],
        flops=10**9,
    )
    grad_field, grad_kernel = call(
        final_body,
        [((cells, NY), BF16), ((OFFSETS * own, channels), F32)],
        final,
        table_y,
        local_back,
        from_low,
        from_high,
        scratch=[eight, wide],
    )
    return (
        grad_field.reshape(own, rows, NY),
        grad_spectral,
        grad_kernel.reshape(OFFSETS, own, channels),
    )


def solution(mesh):
    placed = (
        P("chan", "rows", None),
        P("chan", "rows", None),
        P(None, "chan", None),
        P("rows", None, "chan", None),
        P("rows", None, None),
        P("rows", None),
    )
    return jax.shard_map(
        on_device,
        mesh=mesh,
        in_specs=placed,
        out_specs=(P("chan", "rows", None), P("rows", None, "chan", None), P(None, "chan", None)),
        check_vma=False,
    )
```

time: 178 us -> 159 us (0.89)
  waiting for transfers between devices: 58.8 us -> 40.3 us
  local copies, waits for them, and re-layouts: 18.6 us -> 12.2 us
  Pallas kernels: 11.5 us -> 17.7 us
  starting transfers between devices: 67.9 us -> 71.7 us
  other arithmetic: 4.44 us -> 0.82 us
    all_to_all x6, waiting for transfers between devices: 50.2 us -> 36.3 us  [the longest x4 29.1 us: exchange(): lax.all_to_all(cube, 'rows', split_axis=0, concat_axis=0, tiled=True)]
    pallas_call x9 -> x11, Pallas kernels: 11.5 us -> 17.7 us  [call(): pl.pallas_call(body, out_shape=shapes, in_specs=[pl.BlockSpec(memory_spac...]
    all_to_all x6, starting transfers between devices: 55.6 us -> 60.6 us  [the longest x4 53.3 us: exchange(): lax.all_to_all(cube, 'rows', split_axis=0, concat_axis=0, tiled=True)]
    all_gather x1, waiting for transfers between devices: 4.94 us -> 0.02 us  [on_device(): inputs = lax.all_gather(field_rows, 'chan')]
    reshape x9 -> x4, local copies, waits for them, and re-layouts: 3.57 us -> 0.72 us  [the longest x2 0.37 us: on_device(): got[:, own:own + kernel_lines].reshape(groups, OFFSETS, own, own)]
    concatenate x3 -> x0, other arithmetic: 2.51 us -> none  [the longest x2 1.86 us: with_kernel(): jnp.concatenate([values.reshape(devices, lines, 128), high_part, low_part...]
    unnamed x38 -> x32, local copies, waits for them, and re-layouts: 9.74 us -> 8.49 us
  transfers between devices with their start and end apart: 12 -> 12, of which waited for: 7 -> 8; matrix products, arithmetic and copies ran while one was open for 8% -> 3% of each run, Pallas kernels for 2% -> 5%
where the time goes in v1:
time: 159 us; the launch traced here: 158 us
  starting transfers between devices  71.7 us (45%)
  waiting for transfers between devices  40.3 us (25%)
  Pallas kernels  17.7 us (11%)
  between operations  14.5 us (9%)
  local copies, waits for them, and re-layouts  12.2 us (8%)
    all_to_all x4, starting transfers between devices, exchange(): lax.all_to_all(cube, 'rows', split_axis=0, concat_axis=0, tiled=True)  53.3 us
    all_to_all x4, waiting for transfers between devices, exchange(): lax.all_to_all(cube, 'rows', split_axis=0, concat_axis=0, tiled=True)  29.1 us
    pallas_call x11, Pallas kernels, call(): pl.pallas_call(body, out_shape=shapes, in_specs=[pl.BlockSpec(memory_spac...  17.7 us
    unnamed x32, local copies, waits for them, and re-layouts  8.49 us
    all_to_all x2, starting transfers between devices, swap(): lax.all_to_all(values, 'chan', split_axis=0, concat_axis=0, tiled=True)  7.28 us
    all_to_all x2, waiting for transfers between devices, swap(): lax.all_to_all(values, 'chan', split_axis=0, concat_axis=0, tiled=True)  7.17 us
    ppermute x1, starting transfers between devices, on_device(): low = lax.ppermute(low, 'rows', forward)  3.68 us
    ppermute x1, starting transfers between devices, on_device(): from_low = lax.ppermute(to_high, 'rows', forward)  3.54 us
  transfers between devices with their start and end apart: 12, of which 8 were waited for; matrix products, arithmetic and copies ran while one was open for 3% of the time, Pallas kernels for 5%

profile of v1, /device:TPU:1, one launch (start us, length us, event | category | flops | bytes accessed | tf_op | source)
XLA Modules:
  0.0 157.6 jit_solution(1617578380038724107)
XLA Ops:
  7.3 2.3 %shard_map.121 = (bf16[256,128]{1,0:T(8,128)(2,1)}, bf16[8,32,1024]{2,1,0:T(8,128)(2,1)}) custom-call(bf16[256,1024]{1,0:T(8,128)(2,1)} %bitcast.59, bf16[256,1024]{1,0:T(8,128)(2,1)} %constant.13.clone.table_ref), custom_call_target="tpu_custom_call" | custom-call | flops 100000000 | bytes 589824 | tf_op jit(solution)/shard_map/pallas_call | solution.py:59
  9.6 18.6 %all-to-all-start = ((bf16[128,2,128]{2,1,0:T(2,128)(2,1)}), bf16[128,2,128]{2,1,0:T(2,128)(2,1)S(1)}, u32[]{:S(2)}, u32[]{:S(2)}) async-start(bf16[128,2,128]{2,1,0:T(2,128)(2,1)} %bitcast.63), calls=%async_computation | async-start | bytes 131072 | tf_op jit(solution)/shard_map/all_to_all | solution.py:465
  30.5 9.1 %all-to-all-done = bf16[128,2,128]{2,1,0:T(2,128)(2,1)S(1)} async-done(((bf16[128,2,128]{2,1,0:T(2,128)(2,1)}), bf16[128,2,128]{2,1,0:T(2,128)(2,1)S(1)}, u32[]{:S(2)}, u32[]{:S(2)}) %all-to-all-start) | async-done | bytes 65568 | tf_op jit(solution)/shard_map/all_to_all | solution.py:465
  40.8 4.0 %all-to-all-start.1 = ((bf16[4,112,128]{2,1,0:T(8,128)(2,1)}), bf16[4,112,128]{2,1,0:T(8,128)(2,1)S(1)}, u32[]{:S(2)}, u32[]{:S(2)}) async-start(bf16[4,112,128]{2,1,0:T(8,128)(2,1)} %shard_map.123), calls=%async_computation.1 | async-start | bytes 229376 | tf_op jit(solution)/shard_map/all_to_all | solution.py:469
  45.4 5.6 %all-to-all-done.1.got_ref = bf16[4,112,128]{2,1,0:T(8,128)(2,1)S(1)} async-done(((bf16[4,112,128]{2,1,0:T(8,128)(2,1)}), bf16[4,112,128]{2,1,0:T(8,128)(2,1)S(1)}, u32[]{:S(2)}, u32[]{:S(2)}) %all-to-all-start.1) | async-done | bytes 114720 | tf_op jit(solution)/shard_map/all_to_all | solution.py:469
  52.4 8.1 %all-to-all-start.2 = ((bf16[128,8,128]{2,1,0:T(8,128)(2,1)}), bf16[128,8,128]{2,1,0:T(8,128)(2,1)}, u32[]{:S(2)}, u32[]{:S(2)}) async-start(bf16[128,8,128]{2,1,0:T(8,128)(2,1)} %bitcast.13), calls=%async_computation.2 | async-start | bytes 524288 | tf_op jit(solution)/shard_map/all_to_all | solution.py:465
  60.7 1.6 %copy-done.4 = bf16[32,32,1024]{2,1,0:T(8,128)(2,1)S(1)} copy-done((bf16[32,32,1024]{2,1,0:T(8,128)(2,1)S(1)}, bf16[32,32,1024]{2,1,0:T(8,128)(2,1)}, u32[]{:S(2)}) %copy-start.4) | copy-done | bytes 2097176
  63.1 3.7 %collective-permute-start = (bf16[4,32,1024]{2,1,0:T(8,128)(2,1)}, bf16[4,32,1024]{2,1,0:T(8,128)(2,1)}, u32[]{:S(2)}, u32[]{:S(2)}) collective-permute-start(bf16[4,32,1024]{2,1,0:T(8,128)(2,1)} %get-tuple-element.18), channel_id=1, source_target_pairs={{0,4},{4,8},{8,12},{12,16},{16,20},{20,24},{24,28},{28,32},{32,36}... | collective-permute-start | bytes 786440 | tf_op jit(solution)/shard_map/ppermute | solution.py:537
  66.8 1.9 %collective-permute-start.1 = (bf16[4,32,1024]{2,1,0:T(8,128)(2,1)}, bf16[4,32,1024]{2,1,0:T(8,128)(2,1)}, u32[]{:S(2)}, u32[]{:S(2)}) collective-permute-start(bf16[4,32,1024]{2,1,0:T(8,128)(2,1)} %get-tuple-element.19), channel_id=1, source_target_pairs={{0,508},{4,0},{8,4},{12,8},{16,12},{20,16},{24,20},{28,24},{32,28}... | collective-permute-start | bytes 786440 | tf_op jit(solution)/shard_map/ppermute | solution.py:538
  71.1 4.0 %all-to-all-done.2 = bf16[128,8,128]{2,1,0:T(8,128)(2,1)} async-done(((bf16[128,8,128]{2,1,0:T(8,128)(2,1)}), bf16[128,8,128]{2,1,0:T(8,128)(2,1)}, u32[]{:S(2)}, u32[]{:S(2)}) %all-to-all-start.2) | async-done | bytes 262176 | tf_op jit(solution)/shard_map/all_to_all | solution.py:465
  75.1 1.6 %copy-done.5 = bf16[32,32,1024]{2,1,0:T(8,128)(2,1)S(1)} copy-done((bf16[32,32,1024]{2,1,0:T(8,128)(2,1)S(1)}, bf16[32,32,1024]{2,1,0:T(8,128)(2,1)}, u32[]{:S(2)}) %copy-start.5) | copy-done | bytes 2097176
  78.0 4.3 %shard_map.126 = (bf16[256,1024]{1,0:T(8,128)(2,1)S(1)}, bf16[1024,128]{1,0:T(8,128)(2,1)S(1)}) custom-call(f32[256,1024]{1,0:T(8,128)S(1)} %copy-done.11, bf16[1024,128]{1,0:T(8,128)(2,1)} %bitcast.14.back_ref, bf16[256,1024]{1,0:T(8,128)(2,1)S(1)} %bitcast.49, bf16[256,1024]{1,0:T(8,128)(2,1)S(1)} %copy-done.6, bf16[4,8,32,1024]{3,2,1,0:T(8,128)(2,1)S(1)} %bitcast.47, ...), custom_call_target="tpu_custom_call" | custom-call | flops 2000000000 | bytes 6135808 | tf_op jit(solution)/shard_map/pallas_call | solution.py:59
  83.8 13.6 %all-to-all-start.3 = ((bf16[128,8,128]{2,1,0:T(8,128)(2,1)}), bf16[128,8,128]{2,1,0:T(8,128)(2,1)S(1)}, u32[]{:S(2)}, u32[]{:S(2)}) async-start(bf16[128,8,128]{2,1,0:T(8,128)(2,1)} %bitcast.54), calls=%async_computation.3 | async-start | bytes 524288 | tf_op jit(solution)/shard_map/all_to_all | solution.py:465
  98.1 13.5 %all-to-all-done.3 = bf16[128,8,128]{2,1,0:T(8,128)(2,1)S(1)} async-done(((bf16[128,8,128]{2,1,0:T(8,128)(2,1)}), bf16[128,8,128]{2,1,0:T(8,128)(2,1)S(1)}, u32[]{:S(2)}, u32[]{:S(2)}) %all-to-all-start.3) | async-done | bytes 262176 | tf_op jit(solution)/shard_map/all_to_all | solution.py:465
  111.6 1.8 %shard_map.127 = (bf16[32,128]{1,0:T(8,128)(2,1)S(1)}, bf16[128,128]{1,0:T(8,128)(2,1)}, f32[8,128]{1,0:T(8,128)S(1)}) custom-call(bf16[1024,128]{1,0:T(8,128)(2,1)S(1)} %bitcast.51, bf16[128,2048]{1,0:T(8,128)(2,1)S(1)} %copy-done, bf16[4096,128]{1,0:T(8,128)(2,1)S(1)} %bitcast.44), custom_call_target="tpu_custom_call" | custom-call | flops 100000000 | bytes 1880064 | tf_op jit(solution)/shard_map/pallas_call | solution.py:59
  113.5 3.3 %all-to-all-start.4 = ((bf16[4,32,128]{2,1,0:T(8,128)(2,1)}), bf16[4,32,128]{2,1,0:T(8,128)(2,1)S(1)}, u32[]{:S(2)}, u32[]{:S(2)}) async-start(bf16[4,32,128]{2,1,0:T(8,128)(2,1)} %bitcast.17), calls=%async_computation.4 | async-start | bytes 65536 | tf_op jit(solution)/shard_map/all_to_all | solution.py:469
  119.4 1.6 %all-to-all-done.4.parts_ref = bf16[4,32,128]{2,1,0:T(8,128)(2,1)S(1)} async-done(((bf16[4,32,128]{2,1,0:T(8,128)(2,1)}), bf16[4,32,128]{2,1,0:T(8,128)(2,1)S(1)}, u32[]{:S(2)}, u32[]{:S(2)}) %all-to-all-start.4) | async-done | bytes 32800 | tf_op jit(solution)/shard_map/all_to_all | solution.py:469
  122.2 13.1 %all-to-all-start.5 = ((bf16[128,8,128]{2,1,0:T(8,128)(2,1)}), bf16[128,8,128]{2,1,0:T(8,128)(2,1)S(1)}, u32[]{:S(2)}, u32[]{:S(2)}) async-start(bf16[128,8,128]{2,1,0:T(8,128)(2,1)} %bitcast.24), calls=%async_computation.5 | async-start | bytes 524288 | tf_op jit(solution)/shard_map/all_to_all | solution.py:465
  135.3 1.6 %copy-done.3 = bf16[4,8,32,1024]{3,2,1,0:T(8,128)(2,1)S(1)} copy-done((bf16[4,8,32,1024]{3,2,1,0:T(8,128)(2,1)S(1)}, bf16[4,8,32,1024]{3,2,1,0:T(8,128)(2,1)}, u32[]{:S(2)}) %copy-start.3) | copy-done | bytes 2097176
  137.3 3.5 %collective-permute-start.2 = (bf16[32,1024]{1,0:T(8,128)(2,1)S(1)}, bf16[32,1024]{1,0:T(8,128)(2,1)S(1)}, u32[]{:S(2)}, u32[]{:S(2)}) collective-permute-start(bf16[32,1024]{1,0:T(8,128)(2,1)S(1)} %get-tuple-element.25), channel_id=1, source_target_pairs={{0,4},{4,8},{8,12},{12,16},{16,20},{20,24},{24,28},{28,32},{32,36}... | collective-permute-start | bytes 196616 | tf_op jit(solution)/shard_map/ppermute | solution.py:610
  140.8 1.9 %collective-permute-start.3 = (bf16[32,1024]{1,0:T(8,128)(2,1)S(1)}, bf16[32,1024]{1,0:T(8,128)(2,1)S(1)}, u32[]{:S(2)}, u32[]{:S(2)}) collective-permute-start(bf16[32,1024]{1,0:T(8,128)(2,1)S(1)} %get-tuple-element.26), channel_id=1, source_target_pairs={{0,508},{4,0},{8,4},{12,8},{16,12},{20,16},{24,20},{28,24},{32,28}... | collective-permute-start | bytes 196616 | tf_op jit(solution)/shard_map/ppermute | solution.py:609
  142.8 1.5 shard_map.129.local_ref
  144.3 2.8 %collective-permute-done.3.high_ref = bf16[32,1024]{1,0:T(8,128)(2,1)S(1)} collective-permute-done((bf16[32,1024]{1,0:T(8,128)(2,1)S(1)}, bf16[32,1024]{1,0:T(8,128)(2,1)S(1)}, u32[]{:S(2)}, u32[]{:S(2)}) %collective-permute-start.3) | collective-permute-done | bytes 65568 | tf_op jit(solution)/shard_map/ppermute | solution.py:609
  147.1 2.4 %all-to-all-done.5 = bf16[128,8,128]{2,1,0:T(8,128)(2,1)S(1)} async-done(((bf16[128,8,128]{2,1,0:T(8,128)(2,1)}), bf16[128,8,128]{2,1,0:T(8,128)(2,1)S(1)}, u32[]{:S(2)}, u32[]{:S(2)}) %all-to-all-start.5) | async-done | bytes 262176 | tf_op jit(solution)/shard_map/all_to_all | solution.py:465
  (69 shorter events, 17.8 us)
Async XLA Ops:
  7.2 22.4 %copy-start.9 = (bf16[9,32,128]{2,1,0:T(8,128)(2,1)S(1)}, bf16[9,32,128]{2,1,0:T(8,128)(2,1)}, u32[]{:S(2)}) copy-start(bf16[9,32,128]{2,1,0:T(8,128)(2,1)} %param.12) | copy-start | bytes 221188
  7.2 22.8 %copy-start.15 = (s32[8,16]{1,0:T(8,128)S(1)}, s32[8,16]{1,0:T(8,128)}, u32[]{:S(2)}) copy-start(s32[8,16]{1,0:T(8,128)} %param.15) | copy-start | bytes 1540
  7.2 22.8 %copy-start.14 = (s32[8,16,6]{1,0,2:T(8,128)S(1)}, s32[8,16,6]{1,0,2:T(8,128)}, u32[]{:S(2)}) copy-start(s32[8,16,6]{1,0,2:T(8,128)} %param.14) | copy-start | bytes 9220
  7.2 53.4 %all-gather.6.cloned.1.call-start = ((), (), s32[]{:S(2)}) async-start(), calls=%async_computation.7 | async-start | bytes 2621440 | tf_op jit(solution)/shard_map/all_gather | solution.py:490
  7.2 23.1 %copy-start.12 = (bf16[3,16,1024,1]{2,1,3,0:T(8,128)(2,1)S(1)}, bf16[3,16,1024,1]{2,1,3,0:T(8,128)(2,1)}, u32[]{:S(2)}) copy-start(bf16[3,16,1024,1]{2,1,3,0:T(8,128)(2,1)} %constant.24) | copy-start | bytes 294916
  9.6 30.1 %copy-start = (bf16[128,2048]{1,0:T(8,128)(2,1)S(1)}, bf16[128,2048]{1,0:T(8,128)(2,1)}, u32[]{:S(2)}) copy-start(bf16[128,2048]{1,0:T(8,128)(2,1)} %constant.14.clone.table_ref) | copy-start | bytes 1572868
  9.6 30.0 %all-to-all-start = ((bf16[128,2,128]{2,1,0:T(2,128)(2,1)}), bf16[128,2,128]{2,1,0:T(2,128)(2,1)S(1)}, u32[]{:S(2)}, u32[]{:S(2)}) async-start(bf16[128,2,128]{2,1,0:T(2,128)(2,1)} %bitcast.63), calls=%async_computation | async-start | bytes 131072 | tf_op jit(solution)/shard_map/all_to_all | solution.py:465
  28.2 16.6 %copy-start.13 = (bf16[16,1024]{1,0:T(8,128)(2,1)S(1)}, bf16[16,1024]{1,0:T(8,128)(2,1)}, u32[]{:S(2)}) copy-start(bf16[16,1024]{1,0:T(8,128)(2,1)} %constant.15.clone) | copy-start | bytes 98308
  29.8 21.2 %copy-start.1 = (bf16[1,128,32,128]{3,2,1,0:T(8,128)(2,1)S(1)}, bf16[1,128,32,128]{3,2,1,0:T(8,128)(2,1)}, u32[]{:S(2)}) copy-start(bf16[1,128,32,128]{3,2,1,0:T(8,128)(2,1)} %param.13) | copy-start | bytes 3145732
  40.8 10.2 %all-to-all-start.1 = ((bf16[4,112,128]{2,1,0:T(8,128)(2,1)}), bf16[4,112,128]{2,1,0:T(8,128)(2,1)S(1)}, u32[]{:S(2)}, u32[]{:S(2)}) async-start(bf16[4,112,128]{2,1,0:T(8,128)(2,1)} %shard_map.123), calls=%async_computation.1 | async-start | bytes 229376 | tf_op jit(solution)/shard_map/all_to_all | solution.py:469
  52.4 22.7 %all-to-all-start.2 = ((bf16[128,8,128]{2,1,0:T(8,128)(2,1)}), bf16[128,8,128]{2,1,0:T(8,128)(2,1)}, u32[]{:S(2)}, u32[]{:S(2)}) async-start(bf16[128,8,128]{2,1,0:T(8,128)(2,1)} %bitcast.13), calls=%async_computation.2 | async-start | bytes 524288 | tf_op jit(solution)/shard_map/all_to_all | solution.py:465
  60.6 58.2 %all-gather.4.cloned.1.call-start = ((), (), s32[]{:S(2)}) async-start(), calls=%async_computation.6 | async-start | bytes 2621440 | tf_op jit(solution)/shard_map/all_gather | solution.py:569
  60.7 1.6 %copy-start.4 = (bf16[32,32,1024]{2,1,0:T(8,128)(2,1)S(1)}, bf16[32,32,1024]{2,1,0:T(8,128)(2,1)}, u32[]{:S(2)}) copy-start(bf16[32,32,1024]{2,1,0:T(8,128)(2,1)} %all-gather.6.cloned.1.call-done) | copy-start | bytes 6291460
  63.1 12.0 %copy-start.6 = (bf16[256,1024]{1,0:T(8,128)(2,1)S(1)}, bf16[256,1024]{1,0:T(8,128)(2,1)}, u32[]{:S(2)}) copy-start(bf16[256,1024]{1,0:T(8,128)(2,1)} %constant.13.clone.table_ref) | copy-start | bytes 1572868
  63.1 12.0 %collective-permute-start = (bf16[4,32,1024]{2,1,0:T(8,128)(2,1)}, bf16[4,32,1024]{2,1,0:T(8,128)(2,1)}, u32[]{:S(2)}, u32[]{:S(2)}) collective-permute-start(bf16[4,32,1024]{2,1,0:T(8,128)(2,1)} %get-tuple-element.18), channel_id=1, source_target_pairs={{0,4},{4,8},{8,12},{12,16},{16,20},{20,24},{24,28},{28,32},{32,36}... | collective-permute-start | bytes 786440 | tf_op jit(solution)/shard_map/ppermute | solution.py:537
  66.8 8.3 %collective-permute-start.1 = (bf16[4,32,1024]{2,1,0:T(8,128)(2,1)}, bf16[4,32,1024]{2,1,0:T(8,128)(2,1)}, u32[]{:S(2)}, u32[]{:S(2)}) collective-permute-start(bf16[4,32,1024]{2,1,0:T(8,128)(2,1)} %get-tuple-element.19), channel_id=1, source_target_pairs={{0,508},{4,0},{8,4},{12,8},{16,12},{20,16},{24,20},{28,24},{32,28}... | collective-permute-start | bytes 786440 | tf_op jit(solution)/shard_map/ppermute | solution.py:538
  75.1 1.6 %copy-start.5 = (bf16[32,32,1024]{2,1,0:T(8,128)(2,1)S(1)}, bf16[32,32,1024]{2,1,0:T(8,128)(2,1)}, u32[]{:S(2)}) copy-start(bf16[32,32,1024]{2,1,0:T(8,128)(2,1)} %all-gather.6.cloned.1.call-done) | copy-start | bytes 6291460
  83.8 27.8 %all-to-all-start.3 = ((bf16[128,8,128]{2,1,0:T(8,128)(2,1)}), bf16[128,8,128]{2,1,0:T(8,128)(2,1)S(1)}, u32[]{:S(2)}, u32[]{:S(2)}) async-start(bf16[128,8,128]{2,1,0:T(8,128)(2,1)} %bitcast.54), calls=%async_computation.3 | async-start | bytes 524288 | tf_op jit(solution)/shard_map/all_to_all | solution.py:465
  113.5 7.5 %all-to-all-start.4 = ((bf16[4,32,128]{2,1,0:T(8,128)(2,1)}), bf16[4,32,128]{2,1,0:T(8,128)(2,1)S(1)}, u32[]{:S(2)}, u32[]{:S(2)}) async-start(bf16[4,32,128]{2,1,0:T(8,128)(2,1)} %bitcast.17), calls=%async_computation.4 | async-start | bytes 65536 | tf_op jit(solution)/shard_map/all_to_all | solution.py:469
  117.5 19.7 %copy-start.2 = (bf16[1,128,32,128]{3,2,1,0:T(8,128)(2,1)}, bf16[1,128,32,128]{3,2,1,0:T(8,128)(2,1)S(1)}, u32[]{:S(2)}) copy-start(bf16[1,128,32,128]{3,2,1,0:T(8,128)(2,1)S(1)} %multiply_convert_fusion.refs_1_) | copy-start | bytes 3145732
  122.2 27.3 %all-to-all-start.5 = ((bf16[128,8,128]{2,1,0:T(8,128)(2,1)}), bf16[128,8,128]{2,1,0:T(8,128)(2,1)S(1)}, u32[]{:S(2)}, u32[]{:S(2)}) async-start(bf16[128,8,128]{2,1,0:T(8,128)(2,1)} %bitcast.24), calls=%async_computation.5 | async-start | bytes 524288 | tf_op jit(solution)/shard_map/all_to_all | solution.py:465
  135.3 1.6 %copy-start.3 = (bf16[4,8,32,1024]{3,2,1,0:T(8,128)(2,1)S(1)}, bf16[4,8,32,1024]{3,2,1,0:T(8,128)(2,1)}, u32[]{:S(2)}) copy-start(bf16[4,8,32,1024]{3,2,1,0:T(8,128)(2,1)} %all-gather.4.cloned.1.call-done.grad_ref) | copy-start | bytes 6291460
  137.3 7.0 %collective-permute-start.2 = (bf16[32,1024]{1,0:T(8,128)(2,1)S(1)}, bf16[32,1024]{1,0:T(8,128)(2,1)S(1)}, u32[]{:S(2)}, u32[]{:S(2)}) collective-permute-start(bf16[32,1024]{1,0:T(8,128)(2,1)S(1)} %get-tuple-element.25), channel_id=1, source_target_pairs={{0,4},{4,8},{8,12},{12,16},{16,20},{20,24},{24,28},{28,32},{32,36}... | collective-permute-start | bytes 196616 | tf_op jit(solution)/shard_map/ppermute | solution.py:610
  140.8 6.3 %collective-permute-start.3 = (bf16[32,1024]{1,0:T(8,128)(2,1)S(1)}, bf16[32,1024]{1,0:T(8,128)(2,1)S(1)}, u32[]{:S(2)}, u32[]{:S(2)}) collective-permute-start(bf16[32,1024]{1,0:T(8,128)(2,1)S(1)} %get-tuple-element.26), channel_id=1, source_target_pairs={{0,508},{4,0},{8,4},{12,8},{16,12},{20,16},{24,20},{28,24},{32,28}... | collective-permute-start | bytes 196616 | tf_op jit(solution)/shard_map/ppermute | solution.py:609
  (4 other events, 3.7 us)
Sparse Core Ops, SparseCore 0:
  10.7 42.8 all-gather.5
  83.9 34.7 all-gather.3

commit v2 on v1

--- a/solution.py
+++ b/solution.py
@@ -185,8 +185,7 @@
         part = dot(weight_ref[first * own : (first + step) * own], modes)
         for k in range(step):
             total = jnp.where(lane == first + k, part[k * own : (k + 1) * own], total)
-    line_ref[...] = jnp.zeros(line_ref.shape, F32)
-    write_lines(line_ref, row_values(total, table_ref[...], rows, False), 8)
+    write_lines(line_ref, row_values(total, table_ref[...], rows, False), 2)
     out_ref[...] = line_ref[...].astype(BF16)
 
 
@@ -272,7 +271,7 @@
     rows = field_ref.shape[1]
     channels = kernel_ref.shape[1]
     back_lines[...] = back_ref[...].astype(F32)
-    back = read_lines(back_lines, devices, 8)
+    back = read_lines(back_lines, devices, 2)
     z_ref[...] = local_ref[...] + dot(
         jnp.concatenate([back, back], axis=0), table_ref[...], 0, 0
     )
@@ -516,21 +515,21 @@
     got = swap(sent)
     rows_part = call(
         functools.partial(mix_body, rows=rows),
-        ((8 * devices, 128), BF16),
+        ((2 * devices, 128), BF16),
         weight,
         got,
         table_x,
         masks,
         moved_masks,
         far=(3, 4),
-        scratch=[pltpu.VMEM((8 * devices, 128), F32)],
+        scratch=[two],
     )
     back = exchange(rows_part)
     low, high = call(
         edges_body,
         [((groups, own, NY), BF16)] * 2,
         inputs,
-        rows_part,
+        back,
         far=(0, 1),
         scratch=[pltpu.SemaphoreType.DMA((2,))],
     )
@@ -560,7 +559,7 @@
         kernel_rows,
         scratch=[
             pltpu.VMEM((cells, NY), F32),
-            pltpu.VMEM((8 * devices, 128), F32),
+            two,
             pltpu.VMEM((OFFSETS * own, channels), F32),
             eight,
         ],
@@ -592,10 +591,9 @@
         parts_in,
         table_x,
         kernel_sum,
-        all_grad[0, 0, :16, :128],
         grad_spectral,
         kernel_back,
-        far=(4, 5),
+        far=(3, 4),
         scratch=[eight],
     )
     final = exchange(back_part)
@@ -605,6 +603,7 @@
         kernel_back,
         all_grad,
         masks,
+        flops=10**8,
     )
     from_high = lax.ppermute(to_low, "rows", backward)
     from_low = lax.ppermute(to_high, "rows", forward)

time: 159 us -> 154 us (0.969)
  blocking collectives: 0 us -> 18.1 us
  starting transfers between devices: 71.7 us -> 54.6 us
  local copies, waits for them, and re-layouts: 12.2 us -> 9.53 us
  Pallas kernels: 17.7 us -> 15.1 us
    all_to_all x0 -> x1, blocking collectives: none -> 18.1 us  [exchange(): lax.all_to_all(cube, 'rows', split_axis=0, concat_axis=0, tiled=True)]
    all_to_all x4 -> x3, starting transfers between devices: 53.3 us -> 36.9 us  [exchange(): lax.all_to_all(cube, 'rows', split_axis=0, concat_axis=0, tiled=True)]
    ppermute x1, waiting for transfers between devices: 0.03 us -> 4.6 us  [on_device(): high = lax.ppermute(high, 'rows', backward)]
    unnamed x32 -> x30, local copies, waits for them, and re-layouts: 8.49 us -> 4.72 us
    all_to_all x4 -> x3, waiting for transfers between devices: 29.1 us -> 26.3 us  [exchange(): lax.all_to_all(cube, 'rows', split_axis=0, concat_axis=0, tiled=True)]
    ppermute x1, waiting for transfers between devices: 2.78 us -> 0.01 us  [on_device(): from_high = lax.ppermute(to_low, 'rows', backward)]
    pallas_call x11, Pallas kernels: 17.7 us -> 15.1 us  [call(): pl.pallas_call(body, out_shape=shapes, in_specs=[pl.BlockSpec(memory_spac...]
    all_to_all x2, waiting for transfers between devices: 7.17 us -> 9.05 us  [swap(): lax.all_to_all(values, 'chan', split_axis=0, concat_axis=0, tiled=True)]
  transfers between devices with their start and end apart: 12 -> 11, of which waited for: 8 -> 6; matrix products, arithmetic and copies ran while one was open for 3% -> 4% of each run, Pallas kernels for 5% -> 5%
where the time goes in v2:
time: 154 us; the launch traced here: 153 us
  starting transfers between devices  54.6 us (35%)
  waiting for transfers between devices  40 us (26%)
  blocking collectives  18.1 us (12%)
  Pallas kernels  15.1 us (10%)
  between operations  14.4 us (9%)
  local copies, waits for them, and re-layouts  9.53 us (6%)
    all_to_all x3, starting transfers between devices, exchange(): lax.all_to_all(cube, 'rows', split_axis=0, concat_axis=0, tiled=True)  36.9 us
    all_to_all x3, waiting for transfers between devices, exchange(): lax.all_to_all(cube, 'rows', split_axis=0, concat_axis=0, tiled=True)  26.3 us
    all_to_all x1, blocking collectives, exchange(): lax.all_to_all(cube, 'rows', split_axis=0, concat_axis=0, tiled=True)  18.1 us
    pallas_call x11, Pallas kernels, call(): pl.pallas_call(body, out_shape=shapes, in_specs=[pl.BlockSpec(memory_spac...  15.1 us
    all_to_all x2, waiting for transfers between devices, swap(): lax.all_to_all(values, 'chan', split_axis=0, concat_axis=0, tiled=True)  9.05 us
    all_to_all x2, starting transfers between devices, swap(): lax.all_to_all(values, 'chan', split_axis=0, concat_axis=0, tiled=True)  7.28 us
    unnamed x30, local copies, waits for them, and re-layouts  4.72 us
    ppermute x1, waiting for transfers between devices, on_device(): high = lax.ppermute(high, 'rows', backward)  4.6 us
  transfers between devices with their start and end apart: 11, of which 6 were waited for; matrix products, arithmetic and copies ran while one was open for 4% of the time, Pallas kernels for 5%

profile of v2, /device:TPU:1, one launch (start us, length us, event | category | flops | bytes accessed | tf_op | source)
XLA Modules:
  0.0 153.0 jit_solution(715863335167284505)
XLA Ops:
  7.3 2.3 %shard_map.121 = (bf16[256,128]{1,0:T(8,128)(2,1)}, bf16[8,32,1024]{2,1,0:T(8,128)(2,1)}) custom-call(bf16[256,1024]{1,0:T(8,128)(2,1)} %bitcast.60, bf16[256,1024]{1,0:T(8,128)(2,1)} %constant.13.clone.table_ref), custom_call_target="tpu_custom_call" | custom-call | flops 100000000 | bytes 589824 | tf_op jit(solution)/shard_map/pallas_call | solution.py:59
  9.6 18.6 %all-to-all-start = ((bf16[128,2,128]{2,1,0:T(2,128)(2,1)}), bf16[128,2,128]{2,1,0:T(2,128)(2,1)S(1)}, u32[]{:S(2)}, u32[]{:S(2)}) async-start(bf16[128,2,128]{2,1,0:T(2,128)(2,1)} %bitcast.64), calls=%async_computation | async-start | bytes 131072 | tf_op jit(solution)/shard_map/all_to_all | solution.py:464
  28.2 1.3 copy.41
  30.5 9.1 %all-to-all-done = bf16[128,2,128]{2,1,0:T(2,128)(2,1)S(1)} async-done(((bf16[128,2,128]{2,1,0:T(2,128)(2,1)}), bf16[128,2,128]{2,1,0:T(2,128)(2,1)S(1)}, u32[]{:S(2)}, u32[]{:S(2)}) %all-to-all-start) | async-done | bytes 65568 | tf_op jit(solution)/shard_map/all_to_all | solution.py:464
  40.8 4.0 %all-to-all-start.1 = ((bf16[4,112,128]{2,1,0:T(8,128)(2,1)}), bf16[4,112,128]{2,1,0:T(8,128)(2,1)S(1)}, u32[]{:S(2)}, u32[]{:S(2)}) async-start(bf16[4,112,128]{2,1,0:T(8,128)(2,1)} %shard_map.123), calls=%async_computation.1 | async-start | bytes 229376 | tf_op jit(solution)/shard_map/all_to_all | solution.py:468
  45.4 5.6 %all-to-all-done.1.got_ref = bf16[4,112,128]{2,1,0:T(8,128)(2,1)S(1)} async-done(((bf16[4,112,128]{2,1,0:T(8,128)(2,1)}), bf16[4,112,128]{2,1,0:T(8,128)(2,1)S(1)}, u32[]{:S(2)}, u32[]{:S(2)}) %all-to-all-start.1) | async-done | bytes 114720 | tf_op jit(solution)/shard_map/all_to_all | solution.py:468
  51.7 18.1 %all_to_all.30 = bf16[128,2,128]{2,1,0:T(2,128)(2,1)S(1)} all-to-all(bf16[128,2,128]{2,1,0:T(2,128)(2,1)S(1)} %bitcast.54), channel_id=1, replica_groups=mesh['rows'=128,'chan'=4] {'rows'}, dimensions={0} | all-to-all | bytes 131072 | tf_op jit(solution)/shard_map/all_to_all | solution.py:464
  69.9 1.6 %copy-done.4 = bf16[32,32,1024]{2,1,0:T(8,128)(2,1)S(1)} copy-done((bf16[32,32,1024]{2,1,0:T(8,128)(2,1)S(1)}, bf16[32,32,1024]{2,1,0:T(8,128)(2,1)}, u32[]{:S(2)}) %copy-start.4) | copy-done | bytes 2097176
  71.5 3.0 %collective-permute-start = (bf16[4,32,1024]{2,1,0:T(8,128)(2,1)S(1)}, bf16[4,32,1024]{2,1,0:T(8,128)(2,1)S(1)}, u32[]{:S(2)}, u32[]{:S(2)}) collective-permute-start(bf16[4,32,1024]{2,1,0:T(8,128)(2,1)S(1)} %get-tuple-element.18), channel_id=1, source_target_pairs={{0,4},{4,8},{8,12},{12,16},{16,20},{20,24},{24,28},{28,32},{32,36}... | collective-permute-start | bytes 786440 | tf_op jit(solution)/shard_map/ppermute | solution.py:536
  74.6 1.9 %collective-permute-start.1 = (bf16[4,32,1024]{2,1,0:T(8,128)(2,1)S(1)}, bf16[4,32,1024]{2,1,0:T(8,128)(2,1)S(1)}, u32[]{:S(2)}, u32[]{:S(2)}) collective-permute-start(bf16[4,32,1024]{2,1,0:T(8,128)(2,1)S(1)} %get-tuple-element.19), channel_id=1, source_target_pairs={{0,508},{4,0},{8,4},{12,8},{16,12},{20,16},{24,20},{28,24},{32,28}... | collective-permute-start | bytes 786440 | tf_op jit(solution)/shard_map/ppermute | solution.py:537
  76.5 1.4 shard_map.122.local_ref
  77.9 4.6 %collective-permute-done.1.high_ref = bf16[4,32,1024]{2,1,0:T(8,128)(2,1)S(1)} collective-permute-done((bf16[4,32,1024]{2,1,0:T(8,128)(2,1)S(1)}, bf16[4,32,1024]{2,1,0:T(8,128)(2,1)S(1)}, u32[]{:S(2)}, u32[]{:S(2)}) %collective-permute-start.1) | collective-permute-done | bytes 262176 | tf_op jit(solution)/shard_map/ppermute | solution.py:537
  82.5 3.2 %shard_map.126 = (bf16[256,1024]{1,0:T(8,128)(2,1)S(1)}, bf16[1024,128]{1,0:T(8,128)(2,1)S(1)}) custom-call(f32[256,1024]{1,0:T(8,128)S(1)} %shard_map.122.local_ref, bf16[256,128]{1,0:T(8,128)(2,1)S(1)} %bitcast.52, bf16[256,1024]{1,0:T(8,128)(2,1)S(1)} %bitcast.47, bf16[256,1024]{1,0:T(8,128)(2,1)S(1)} %copy-done.6, bf16[4,8,32,1024]{3,2,1,0:T(8,128)(2,1)S(1)} %bitcast.45, ...), custom_call_target="tpu_custom_call" | custom-call | flops 2000000000 | bytes 5939200 | tf_op jit(solution)/shard_map/pallas_call | solution.py:59
  87.3 10.3 %all-to-all-start.3 = ((bf16[128,8,128]{2,1,0:T(8,128)(2,1)}), bf16[128,8,128]{2,1,0:T(8,128)(2,1)S(1)}, u32[]{:S(2)}, u32[]{:S(2)}) async-start(bf16[128,8,128]{2,1,0:T(8,128)(2,1)} %bitcast.55), calls=%async_computation.3 | async-start | bytes 524288 | tf_op jit(solution)/shard_map/all_to_all | solution.py:464
  100.0 11.8 %all-to-all-done.3 = bf16[128,8,128]{2,1,0:T(8,128)(2,1)S(1)} async-done(((bf16[128,8,128]{2,1,0:T(8,128)(2,1)}), bf16[128,8,128]{2,1,0:T(8,128)(2,1)S(1)}, u32[]{:S(2)}, u32[]{:S(2)}) %all-to-all-start.3) | async-done | bytes 262176 | tf_op jit(solution)/shard_map/all_to_all | solution.py:464
  111.8 1.8 %shard_map.127 = (bf16[32,128]{1,0:T(8,128)(2,1)S(1)}, bf16[128,128]{1,0:T(8,128)(2,1)}, f32[8,128]{1,0:T(8,128)S(1)}) custom-call(bf16[1024,128]{1,0:T(8,128)(2,1)S(1)} %bitcast.49, bf16[128,2048]{1,0:T(8,128)(2,1)S(1)} %copy-done, bf16[4096,128]{1,0:T(8,128)(2,1)S(1)} %bitcast.42), custom_call_target="tpu_custom_call" | custom-call | flops 100000000 | bytes 1880064 | tf_op jit(solution)/shard_map/pallas_call | solution.py:59
  113.7 3.3 %all-to-all-start.4 = ((bf16[4,32,128]{2,1,0:T(8,128)(2,1)}), bf16[4,32,128]{2,1,0:T(8,128)(2,1)S(1)}, u32[]{:S(2)}, u32[]{:S(2)}) async-start(bf16[4,32,128]{2,1,0:T(8,128)(2,1)} %bitcast.17), calls=%async_computation.4 | async-start | bytes 65536 | tf_op jit(solution)/shard_map/all_to_all | solution.py:468
  117.7 3.5 %all-to-all-done.4.parts_ref = bf16[4,32,128]{2,1,0:T(8,128)(2,1)S(1)} async-done(((bf16[4,32,128]{2,1,0:T(8,128)(2,1)}), bf16[4,32,128]{2,1,0:T(8,128)(2,1)S(1)}, u32[]{:S(2)}, u32[]{:S(2)}) %all-to-all-start.4) | async-done | bytes 32800 | tf_op jit(solution)/shard_map/all_to_all | solution.py:468
  122.5 8.1 %all-to-all-start.5 = ((bf16[128,8,128]{2,1,0:T(8,128)(2,1)}), bf16[128,8,128]{2,1,0:T(8,128)(2,1)S(1)}, u32[]{:S(2)}, u32[]{:S(2)}) async-start(bf16[128,8,128]{2,1,0:T(8,128)(2,1)} %bitcast.22), calls=%async_computation.5 | async-start | bytes 524288 | tf_op jit(solution)/shard_map/all_to_all | solution.py:464
  130.6 1.6 %copy-done.3 = bf16[4,8,32,1024]{3,2,1,0:T(8,128)(2,1)S(1)} copy-done((bf16[4,8,32,1024]{3,2,1,0:T(8,128)(2,1)S(1)}, bf16[4,8,32,1024]{3,2,1,0:T(8,128)(2,1)}, u32[]{:S(2)}) %copy-start.3) | copy-done | bytes 2097176
  132.6 3.5 %collective-permute-start.2 = (bf16[32,1024]{1,0:T(8,128)(2,1)S(1)}, bf16[32,1024]{1,0:T(8,128)(2,1)S(1)}, u32[]{:S(2)}, u32[]{:S(2)}) collective-permute-start(bf16[32,1024]{1,0:T(8,128)(2,1)S(1)} %get-tuple-element.25), channel_id=1, source_target_pairs={{0,4},{4,8},{8,12},{12,16},{16,20},{20,24},{24,28},{28,32},{32,36}... | collective-permute-start | bytes 196616 | tf_op jit(solution)/shard_map/ppermute | solution.py:609
  136.1 1.9 %collective-permute-start.3 = (bf16[32,1024]{1,0:T(8,128)(2,1)S(1)}, bf16[32,1024]{1,0:T(8,128)(2,1)S(1)}, u32[]{:S(2)}, u32[]{:S(2)}) collective-permute-start(bf16[32,1024]{1,0:T(8,128)(2,1)S(1)} %get-tuple-element.26), channel_id=1, source_target_pairs={{0,508},{4,0},{8,4},{12,8},{16,12},{20,16},{24,20},{28,24},{32,28}... | collective-permute-start | bytes 196616 | tf_op jit(solution)/shard_map/ppermute | solution.py:608
  138.0 1.5 shard_map.129.local_ref
  139.6 5.3 %all-to-all-done.5 = bf16[128,8,128]{2,1,0:T(8,128)(2,1)S(1)} async-done(((bf16[128,8,128]{2,1,0:T(8,128)(2,1)}), bf16[128,8,128]{2,1,0:T(8,128)(2,1)S(1)}, u32[]{:S(2)}, u32[]{:S(2)}) %all-to-all-start.5) | async-done | bytes 262176 | tf_op jit(solution)/shard_map/all_to_all | solution.py:464
  (65 shorter events, 11.1 us)
Async XLA Ops:
  7.2 22.4 %copy-start.9 = (bf16[9,32,128]{2,1,0:T(8,128)(2,1)S(1)}, bf16[9,32,128]{2,1,0:T(8,128)(2,1)}, u32[]{:S(2)}) copy-start(bf16[9,32,128]{2,1,0:T(8,128)(2,1)} %param.12) | copy-start | bytes 221188
  7.2 22.8 %copy-start.14 = (s32[8,16]{1,0:T(8,128)S(1)}, s32[8,16]{1,0:T(8,128)}, u32[]{:S(2)}) copy-start(s32[8,16]{1,0:T(8,128)} %param.15) | copy-start | bytes 1540
  7.2 22.8 %copy-start.13 = (s32[8,16,6]{1,0,2:T(8,128)S(1)}, s32[8,16,6]{1,0,2:T(8,128)}, u32[]{:S(2)}) copy-start(s32[8,16,6]{1,0,2:T(8,128)} %param.14) | copy-start | bytes 9220
  7.2 62.7 %all-gather.6.cloned.1.call-start = ((), (), s32[]{:S(2)}) async-start(), calls=%async_computation.7 | async-start | bytes 2621440 | tf_op jit(solution)/shard_map/all_gather | solution.py:489
  7.2 23.1 %copy-start.11 = (bf16[3,16,1024,1]{2,1,3,0:T(8,128)(2,1)S(1)}, bf16[3,16,1024,1]{2,1,3,0:T(8,128)(2,1)}, u32[]{:S(2)}) copy-start(bf16[3,16,1024,1]{2,1,3,0:T(8,128)(2,1)} %constant.24) | copy-start | bytes 294916
  9.6 30.1 %copy-start = (bf16[128,2048]{1,0:T(8,128)(2,1)S(1)}, bf16[128,2048]{1,0:T(8,128)(2,1)}, u32[]{:S(2)}) copy-start(bf16[128,2048]{1,0:T(8,128)(2,1)} %constant.14.clone.table_ref) | copy-start | bytes 1572868
  9.6 30.0 %all-to-all-start = ((bf16[128,2,128]{2,1,0:T(2,128)(2,1)}), bf16[128,2,128]{2,1,0:T(2,128)(2,1)S(1)}, u32[]{:S(2)}, u32[]{:S(2)}) async-start(bf16[128,2,128]{2,1,0:T(2,128)(2,1)} %bitcast.64), calls=%async_computation | async-start | bytes 131072 | tf_op jit(solution)/shard_map/all_to_all | solution.py:464
  28.2 16.6 %copy-start.12 = (bf16[16,1024]{1,0:T(8,128)(2,1)S(1)}, bf16[16,1024]{1,0:T(8,128)(2,1)}, u32[]{:S(2)}) copy-start(bf16[16,1024]{1,0:T(8,128)(2,1)} %constant.15.clone) | copy-start | bytes 98308
  29.8 21.2 %copy-start.1 = (bf16[1,128,32,128]{3,2,1,0:T(8,128)(2,1)S(1)}, bf16[1,128,32,128]{3,2,1,0:T(8,128)(2,1)}, u32[]{:S(2)}) copy-start(bf16[1,128,32,128]{3,2,1,0:T(8,128)(2,1)} %param.13) | copy-start | bytes 3145732
  40.8 10.2 %all-to-all-start.1 = ((bf16[4,112,128]{2,1,0:T(8,128)(2,1)}), bf16[4,112,128]{2,1,0:T(8,128)(2,1)S(1)}, u32[]{:S(2)}, u32[]{:S(2)}) async-start(bf16[4,112,128]{2,1,0:T(8,128)(2,1)} %shard_map.123), calls=%async_computation.1 | async-start | bytes 229376 | tf_op jit(solution)/shard_map/all_to_all | solution.py:468
  44.8 85.8 %all-gather.4.cloned.1.call-start = ((), (), s32[]{:S(2)}) async-start(), calls=%async_computation.6 | async-start | bytes 2621440 | tf_op jit(solution)/shard_map/all_gather | solution.py:568
  51.0 25.5 %copy-start.10 = (bf16[9,32,128]{2,1,0:T(8,128)(2,1)S(1)}, bf16[9,32,128]{2,1,0:T(8,128)(2,1)}, u32[]{:S(2)}) copy-start(bf16[9,32,128]{2,1,0:T(8,128)(2,1)} %param.12) | copy-start | bytes 221188
  69.9 1.6 %copy-start.4 = (bf16[32,32,1024]{2,1,0:T(8,128)(2,1)S(1)}, bf16[32,32,1024]{2,1,0:T(8,128)(2,1)}, u32[]{:S(2)}) copy-start(bf16[32,32,1024]{2,1,0:T(8,128)(2,1)} %all-gather.6.cloned.1.call-done) | copy-start | bytes 6291460
  71.5 5.0 %copy-start.5 = (bf16[32,32,1024]{2,1,0:T(8,128)(2,1)S(1)}, bf16[32,32,1024]{2,1,0:T(8,128)(2,1)}, u32[]{:S(2)}) copy-start(bf16[32,32,1024]{2,1,0:T(8,128)(2,1)} %all-gather.6.cloned.1.call-done) | copy-start | bytes 6291460
  71.5 11.0 %copy-start.6 = (bf16[256,1024]{1,0:T(8,128)(2,1)S(1)}, bf16[256,1024]{1,0:T(8,128)(2,1)}, u32[]{:S(2)}) copy-start(bf16[256,1024]{1,0:T(8,128)(2,1)} %constant.13.clone.table_ref) | copy-start | bytes 1572868
  71.5 6.4 %collective-permute-start = (bf16[4,32,1024]{2,1,0:T(8,128)(2,1)S(1)}, bf16[4,32,1024]{2,1,0:T(8,128)(2,1)S(1)}, u32[]{:S(2)}, u32[]{:S(2)}) collective-permute-start(bf16[4,32,1024]{2,1,0:T(8,128)(2,1)S(1)} %get-tuple-element.18), channel_id=1, source_target_pairs={{0,4},{4,8},{8,12},{12,16},{16,20},{20,24},{24,28},{28,32},{32,36}... | collective-permute-start | bytes 786440 | tf_op jit(solution)/shard_map/ppermute | solution.py:536
  74.6 8.0 %collective-permute-start.1 = (bf16[4,32,1024]{2,1,0:T(8,128)(2,1)S(1)}, bf16[4,32,1024]{2,1,0:T(8,128)(2,1)S(1)}, u32[]{:S(2)}, u32[]{:S(2)}) collective-permute-start(bf16[4,32,1024]{2,1,0:T(8,128)(2,1)S(1)} %get-tuple-element.19), channel_id=1, source_target_pairs={{0,508},{4,0},{8,4},{12,8},{16,12},{20,16},{24,20},{28,24},{32,28}... | collective-permute-start | bytes 786440 | tf_op jit(solution)/shard_map/ppermute | solution.py:537
  87.3 24.5 %all-to-all-start.3 = ((bf16[128,8,128]{2,1,0:T(8,128)(2,1)}), bf16[128,8,128]{2,1,0:T(8,128)(2,1)S(1)}, u32[]{:S(2)}, u32[]{:S(2)}) async-start(bf16[128,8,128]{2,1,0:T(8,128)(2,1)} %bitcast.55), calls=%async_computation.3 | async-start | bytes 524288 | tf_op jit(solution)/shard_map/all_to_all | solution.py:464
  113.7 7.5 %all-to-all-start.4 = ((bf16[4,32,128]{2,1,0:T(8,128)(2,1)}), bf16[4,32,128]{2,1,0:T(8,128)(2,1)S(1)}, u32[]{:S(2)}, u32[]{:S(2)}) async-start(bf16[4,32,128]{2,1,0:T(8,128)(2,1)} %bitcast.17), calls=%async_computation.4 | async-start | bytes 65536 | tf_op jit(solution)/shard_map/all_to_all | solution.py:468
  117.7 14.8 %copy-start.2 = (bf16[1,128,32,128]{3,2,1,0:T(8,128)(2,1)}, bf16[1,128,32,128]{3,2,1,0:T(8,128)(2,1)S(1)}, u32[]{:S(2)}) copy-start(bf16[1,128,32,128]{3,2,1,0:T(8,128)(2,1)S(1)} %multiply_convert_fusion.refs_0_) | copy-start | bytes 3145732
  122.5 22.5 %all-to-all-start.5 = ((bf16[128,8,128]{2,1,0:T(8,128)(2,1)}), bf16[128,8,128]{2,1,0:T(8,128)(2,1)S(1)}, u32[]{:S(2)}, u32[]{:S(2)}) async-start(bf16[128,8,128]{2,1,0:T(8,128)(2,1)} %bitcast.22), calls=%async_computation.5 | async-start | bytes 524288 | tf_op jit(solution)/shard_map/all_to_all | solution.py:464
  130.6 1.6 %copy-start.3 = (bf16[4,8,32,1024]{3,2,1,0:T(8,128)(2,1)S(1)}, bf16[4,8,32,1024]{3,2,1,0:T(8,128)(2,1)}, u32[]{:S(2)}) copy-start(bf16[4,8,32,1024]{3,2,1,0:T(8,128)(2,1)} %all-gather.4.cloned.1.call-done.grad_ref) | copy-start | bytes 6291460
  132.6 12.4 %collective-permute-start.2 = (bf16[32,1024]{1,0:T(8,128)(2,1)S(1)}, bf16[32,1024]{1,0:T(8,128)(2,1)S(1)}, u32[]{:S(2)}, u32[]{:S(2)}) collective-permute-start(bf16[32,1024]{1,0:T(8,128)(2,1)S(1)} %get-tuple-element.25), channel_id=1, source_target_pairs={{0,4},{4,8},{8,12},{12,16},{16,20},{20,24},{24,28},{28,32},{32,36}... | collective-permute-start | bytes 196616 | tf_op jit(solution)/shard_map/ppermute | solution.py:609
  136.1 8.8 %collective-permute-start.3 = (bf16[32,1024]{1,0:T(8,128)(2,1)S(1)}, bf16[32,1024]{1,0:T(8,128)(2,1)S(1)}, u32[]{:S(2)}, u32[]{:S(2)}) collective-permute-start(bf16[32,1024]{1,0:T(8,128)(2,1)S(1)} %get-tuple-element.26), channel_id=1, source_target_pairs={{0,508},{4,0},{8,4},{12,8},{16,12},{20,16},{24,20},{28,24},{32,28}... | collective-permute-start | bytes 196616 | tf_op jit(solution)/shard_map/ppermute | solution.py:608
  (2 other events, 1.5 us)
Sparse Core Ops, SparseCore 0:
  10.7 42.8 all-gather.5
  87.4 31.6 all-gather.3

commit v3 on v2

--- a/solution.py
+++ b/solution.py
@@ -290,7 +290,11 @@
     pre_ref[...] = grad_low
     write_lines(line_ref, column_spread(grad_low, table_ref[...]), 8)
     grad = grad_low.astype(F32)
-    shifted = [pltpu.roll(grad, NY - 1, 1), grad, pltpu.roll(grad, 1, 1)]
+    shifted = [
+        pltpu.roll(grad, NY - 1, 1).astype(BF16),
+        grad_low,
+        pltpu.roll(grad, 1, 1).astype(BF16),
+    ]
     total = [jnp.zeros((3 * own, channels), F32) for _ in range(3)]
     for j in range(-1, rows + 1):
         ref = low_ref if j < 0 else high_ref if j == rows else field_ref.at[:, j]
@@ -303,10 +307,8 @@
             for k in range(3):
                 t = 3 * group + k
                 pieces.append(
-                    (
-                        shifted[k][x * own : (x + 1) * own]
-                        * mask_ref[x * OFFSETS + t : x * OFFSETS + t + 1]
-                    ).astype(BF16)
+                    shifted[k][x * own : (x + 1) * own]
+                    * mask_ref[x * OFFSETS + t : x * OFFSETS + t + 1].astype(BF16)
                 )
             total[group] = total[group] + dot(jnp.concatenate(pieces, axis=0), source, 1, 1)
     for group in range(3):
@@ -356,14 +358,12 @@
     for k in range(1, parts.shape[0]):
         total = total + parts[k]
     devices = table_ref.shape[0]
-    write_lines(line_ref, row_values(total, table_ref[...], rows, True), 8)
-    shares = [
-        jnp.broadcast_to(
+    write_lines(line_ref, row_values(total, table_ref[...], rows, True), 6)
+    for k in range(3):
+        every(line_ref, 2 + k, devices, 6)[...] = jnp.broadcast_to(
             sum_ref[2 + k : 3 + k] + sum_ref[5 + k : 6 + k], (devices, sum_ref.shape[1])
         )
-        for k in range(3)
-    ]
-    write_shares(line_ref, shares, 8, devices, devices)
+    every(line_ref, 5, devices, 6)[...] = jnp.zeros((devices, sum_ref.shape[1]), F32)
     out_ref[...] = line_ref[...].astype(BF16)
 
 
@@ -417,7 +417,7 @@
     devices = table_ref.shape[0] // 2
     holders = share_ref.shape[0] // 3
     line_ref[...] = moved_ref[...].astype(F32)
-    back = read_lines(line_ref, devices, 8)
+    back = read_lines(line_ref, devices, 6)
     for x, ref in ((0, low_ref), (rows - 1, high_ref)):
         edge = ref[...].astype(F32)
         for k, view in enumerate(wide_rows(sum_ref, x, own, rows)):
@@ -428,9 +428,7 @@
     spectral = dot(jnp.concatenate([back, back], axis=0), table_ref[...], 0, 0)
     out_ref[...] = (spectral + get_wide(local_ref) + get_wide(sum_ref)).astype(BF16)
     for k in range(3):
-        every(share_ref, k, holders, 3)[...] = (
-            every(line_ref, 2 + k, holders, 8)[...] + every(line_ref, 5 + k, holders, 8)[...]
-        )
+        every(share_ref, k, holders, 3)[...] = every(line_ref, 2 + k, holders, 6)[...]
 
 
 def tile_masks(tile_ids, tile_counts):
@@ -460,7 +458,8 @@
     forward = [(i, (i + 1) % devices) for i in range(devices)]
     backward = [(i, (i - 1) % devices) for i in range(devices)]
     def exchange(lines):
-        cube = lines.reshape(devices, -1, 128)
+        count = lines.shape[0] // devices
+        cube = lines.reshape(-1, count if count % 8 == 0 else 2, 128)
         moved = lax.all_to_all(cube, "rows", split_axis=0, concat_axis=0, tiled=True)
         return moved.reshape(lines.shape)
 
@@ -469,6 +468,7 @@
 
     weight = spectral_weight.reshape(waves * own, channels)
     two = pltpu.VMEM((2 * devices, 128), F32)
+    six = pltpu.VMEM((6 * devices, 128), F32)
     eight = pltpu.VMEM((8 * devices, 128), F32)
     wide = pltpu.VMEM((NY // 128, cells, 128), F32)
     spread, field_rows = call(
@@ -587,14 +587,14 @@
     grad_spectral = (left[None, :, :, None] * right[None, :, None, :]).astype(BF16)
     back_part = call(
         functools.partial(back_rows_body, rows=rows),
-        ((8 * devices, 128), BF16),
+        ((6 * devices, 128), BF16),
         parts_in,
         table_x,
         kernel_sum,
         grad_spectral,
         kernel_back,
         far=(3, 4),
-        scratch=[eight],
+        scratch=[six],
     )
     final = exchange(back_part)
     to_low, to_high = call(
@@ -624,7 +624,7 @@
         local_back,
         from_low,
         from_high,
-        scratch=[eight, wide],
+        scratch=[six, wide],
     )
     return (
         grad_field.reshape(own, rows, NY),

time: 154 us -> 153 us (level)
  no operation moved by 1% of the time
where the time goes in v3:
time: 153 us; the launch traced here: 152 us
  starting transfers between devices  54.7 us (36%)
  waiting for transfers between devices  38.9 us (25%)
  blocking collectives  18.1 us (12%)
  Pallas kernels  15 us (10%)
  between operations  14.4 us (9%)
  local copies, waits for them, and re-layouts  9.53 us (6%)
    all_to_all x3, starting transfers between devices, exchange(): lax.all_to_all(cube, 'rows', split_axis=0, concat_axis=0, tiled=True)  36.9 us
    all_to_all x3, waiting for transfers between devices, exchange(): lax.all_to_all(cube, 'rows', split_axis=0, concat_axis=0, tiled=True)  25.1 us
    all_to_all x1, blocking collectives, exchange(): lax.all_to_all(cube, 'rows', split_axis=0, concat_axis=0, tiled=True)  18.1 us
    pallas_call x11, Pallas kernels, call(): pl.pallas_call(body, out_shape=shapes, in_specs=[pl.BlockSpec(memory_spac...  15 us
    all_to_all x2, waiting for transfers between devices, swap(): lax.all_to_all(values, 'chan', split_axis=0, concat_axis=0, tiled=True)  9.05 us
    all_to_all x2, starting transfers between devices, swap(): lax.all_to_all(values, 'chan', split_axis=0, concat_axis=0, tiled=True)  7.28 us
    unnamed x30, local copies, waits for them, and re-layouts  4.72 us
    ppermute x1, waiting for transfers between devices, on_device(): high = lax.ppermute(high, 'rows', backward)  4.6 us
  transfers between devices with their start and end apart: 11, of which 6 were waited for; matrix products, arithmetic and copies ran while one was open for 4% of the time, Pallas kernels for 5%

profile of v3, /device:TPU:1, one launch (start us, length us, event | category | flops | bytes accessed | tf_op | source)
XLA Modules:
  0.0 151.8 jit_solution(12495591700614468519)
XLA Ops:
  7.3 2.3 %shard_map.121 = (bf16[256,128]{1,0:T(8,128)(2,1)}, bf16[8,32,1024]{2,1,0:T(8,128)(2,1)}) custom-call(bf16[256,1024]{1,0:T(8,128)(2,1)} %bitcast.60, bf16[256,1024]{1,0:T(8,128)(2,1)} %constant.13.clone.table_ref), custom_call_target="tpu_custom_call" | custom-call | flops 100000000 | bytes 589824 | tf_op jit(solution)/shard_map/pallas_call | solution.py:59
  9.6 18.6 %all-to-all-start = ((bf16[128,2,128]{2,1,0:T(2,128)(2,1)}), bf16[128,2,128]{2,1,0:T(2,128)(2,1)S(1)}, u32[]{:S(2)}, u32[]{:S(2)}) async-start(bf16[128,2,128]{2,1,0:T(2,128)(2,1)} %bitcast.64), calls=%async_computation | async-start | bytes 131072 | tf_op jit(solution)/shard_map/all_to_all | solution.py:463
  28.2 1.3 copy.41
  30.5 9.1 %all-to-all-done = bf16[128,2,128]{2,1,0:T(2,128)(2,1)S(1)} async-done(((bf16[128,2,128]{2,1,0:T(2,128)(2,1)}), bf16[128,2,128]{2,1,0:T(2,128)(2,1)S(1)}, u32[]{:S(2)}, u32[]{:S(2)}) %all-to-all-start) | async-done | bytes 65568 | tf_op jit(solution)/shard_map/all_to_all | solution.py:463
  40.8 4.0 %all-to-all-start.1 = ((bf16[4,112,128]{2,1,0:T(8,128)(2,1)}), bf16[4,112,128]{2,1,0:T(8,128)(2,1)S(1)}, u32[]{:S(2)}, u32[]{:S(2)}) async-start(bf16[4,112,128]{2,1,0:T(8,128)(2,1)} %shard_map.123), calls=%async_computation.1 | async-start | bytes 229376 | tf_op jit(solution)/shard_map/all_to_all | solution.py:467
  45.4 5.6 %all-to-all-done.1.got_ref = bf16[4,112,128]{2,1,0:T(8,128)(2,1)S(1)} async-done(((bf16[4,112,128]{2,1,0:T(8,128)(2,1)}), bf16[4,112,128]{2,1,0:T(8,128)(2,1)S(1)}, u32[]{:S(2)}, u32[]{:S(2)}) %all-to-all-start.1) | async-done | bytes 114720 | tf_op jit(solution)/shard_map/all_to_all | solution.py:467
  51.7 18.1 %all_to_all.30 = bf16[128,2,128]{2,1,0:T(2,128)(2,1)S(1)} all-to-all(bf16[128,2,128]{2,1,0:T(2,128)(2,1)S(1)} %bitcast.54), channel_id=1, replica_groups=mesh['rows'=128,'chan'=4] {'rows'}, dimensions={0} | all-to-all | bytes 131072 | tf_op jit(solution)/shard_map/all_to_all | solution.py:463
  69.9 1.6 %copy-done.4 = bf16[32,32,1024]{2,1,0:T(8,128)(2,1)S(1)} copy-done((bf16[32,32,1024]{2,1,0:T(8,128)(2,1)S(1)}, bf16[32,32,1024]{2,1,0:T(8,128)(2,1)}, u32[]{:S(2)}) %copy-start.4) | copy-done | bytes 2097176
  71.5 3.0 %collective-permute-start = (bf16[4,32,1024]{2,1,0:T(8,128)(2,1)S(1)}, bf16[4,32,1024]{2,1,0:T(8,128)(2,1)S(1)}, u32[]{:S(2)}, u32[]{:S(2)}) collective-permute-start(bf16[4,32,1024]{2,1,0:T(8,128)(2,1)S(1)} %get-tuple-element.18), channel_id=1, source_target_pairs={{0,4},{4,8},{8,12},{12,16},{16,20},{20,24},{24,28},{28,32},{32,36}... | collective-permute-start | bytes 786440 | tf_op jit(solution)/shard_map/ppermute | solution.py:536
  74.6 1.9 %collective-permute-start.1 = (bf16[4,32,1024]{2,1,0:T(8,128)(2,1)S(1)}, bf16[4,32,1024]{2,1,0:T(8,128)(2,1)S(1)}, u32[]{:S(2)}, u32[]{:S(2)}) collective-permute-start(bf16[4,32,1024]{2,1,0:T(8,128)(2,1)S(1)} %get-tuple-element.19), channel_id=1, source_target_pairs={{0,508},{4,0},{8,4},{12,8},{16,12},{20,16},{24,20},{28,24},{32,28}... | collective-permute-start | bytes 786440 | tf_op jit(solution)/shard_map/ppermute | solution.py:537
  76.5 1.4 shard_map.122.local_ref
  77.9 4.6 %collective-permute-done.1.high_ref = bf16[4,32,1024]{2,1,0:T(8,128)(2,1)S(1)} collective-permute-done((bf16[4,32,1024]{2,1,0:T(8,128)(2,1)S(1)}, bf16[4,32,1024]{2,1,0:T(8,128)(2,1)S(1)}, u32[]{:S(2)}, u32[]{:S(2)}) %collective-permute-start.1) | collective-permute-done | bytes 262176 | tf_op jit(solution)/shard_map/ppermute | solution.py:537
  82.5 3.2 %shard_map.126 = (bf16[256,1024]{1,0:T(8,128)(2,1)S(1)}, bf16[1024,128]{1,0:T(8,128)(2,1)S(1)}) custom-call(f32[256,1024]{1,0:T(8,128)S(1)} %shard_map.122.local_ref, bf16[256,128]{1,0:T(8,128)(2,1)S(1)} %bitcast.52, bf16[256,1024]{1,0:T(8,128)(2,1)S(1)} %bitcast.47, bf16[256,1024]{1,0:T(8,128)(2,1)S(1)} %copy-done.6, bf16[4,8,32,1024]{3,2,1,0:T(8,128)(2,1)S(1)} %bitcast.45, ...), custom_call_target="tpu_custom_call" | custom-call | flops 2000000000 | bytes 5939200 | tf_op jit(solution)/shard_map/pallas_call | solution.py:59
  87.3 10.3 %all-to-all-start.3 = ((bf16[128,8,128]{2,1,0:T(8,128)(2,1)}), bf16[128,8,128]{2,1,0:T(8,128)(2,1)S(1)}, u32[]{:S(2)}, u32[]{:S(2)}) async-start(bf16[128,8,128]{2,1,0:T(8,128)(2,1)} %bitcast.55), calls=%async_computation.3 | async-start | bytes 524288 | tf_op jit(solution)/shard_map/all_to_all | solution.py:463
  100.0 11.8 %all-to-all-done.3 = bf16[128,8,128]{2,1,0:T(8,128)(2,1)S(1)} async-done(((bf16[128,8,128]{2,1,0:T(8,128)(2,1)}), bf16[128,8,128]{2,1,0:T(8,128)(2,1)S(1)}, u32[]{:S(2)}, u32[]{:S(2)}) %all-to-all-start.3) | async-done | bytes 262176 | tf_op jit(solution)/shard_map/all_to_all | solution.py:463
  111.8 1.8 %shard_map.127 = (bf16[32,128]{1,0:T(8,128)(2,1)S(1)}, bf16[128,128]{1,0:T(8,128)(2,1)}, f32[8,128]{1,0:T(8,128)S(1)}) custom-call(bf16[1024,128]{1,0:T(8,128)(2,1)S(1)} %bitcast.48, bf16[128,2048]{1,0:T(8,128)(2,1)S(1)} %copy-done, bf16[4096,128]{1,0:T(8,128)(2,1)S(1)} %bitcast.42), custom_call_target="tpu_custom_call" | custom-call | flops 100000000 | bytes 1880064 | tf_op jit(solution)/shard_map/pallas_call | solution.py:59
  113.7 3.3 %all-to-all-start.4 = ((bf16[4,32,128]{2,1,0:T(8,128)(2,1)}), bf16[4,32,128]{2,1,0:T(8,128)(2,1)S(1)}, u32[]{:S(2)}, u32[]{:S(2)}) async-start(bf16[4,32,128]{2,1,0:T(8,128)(2,1)} %bitcast.17), calls=%async_computation.4 | async-start | bytes 65536 | tf_op jit(solution)/shard_map/all_to_all | solution.py:467
  117.7 3.5 %all-to-all-done.4.parts_ref = bf16[4,32,128]{2,1,0:T(8,128)(2,1)S(1)} async-done(((bf16[4,32,128]{2,1,0:T(8,128)(2,1)}), bf16[4,32,128]{2,1,0:T(8,128)(2,1)S(1)}, u32[]{:S(2)}, u32[]{:S(2)}) %all-to-all-start.4) | async-done | bytes 32800 | tf_op jit(solution)/shard_map/all_to_all | solution.py:467
  122.4 8.1 %all-to-all-start.5 = ((bf16[384,2,128]{2,1,0:T(2,128)(2,1)}), bf16[384,2,128]{2,1,0:T(2,128)(2,1)S(1)}, u32[]{:S(2)}, u32[]{:S(2)}) async-start(bf16[384,2,128]{2,1,0:T(2,128)(2,1)} %bitcast.22), calls=%async_computation.5 | async-start | bytes 393216 | tf_op jit(solution)/shard_map/all_to_all | solution.py:463
  130.5 1.6 %copy-done.3 = bf16[4,8,32,1024]{3,2,1,0:T(8,128)(2,1)S(1)} copy-done((bf16[4,8,32,1024]{3,2,1,0:T(8,128)(2,1)S(1)}, bf16[4,8,32,1024]{3,2,1,0:T(8,128)(2,1)}, u32[]{:S(2)}) %copy-start.3) | copy-done | bytes 2097176
  132.5 3.5 %collective-permute-start.2 = (bf16[32,1024]{1,0:T(8,128)(2,1)S(1)}, bf16[32,1024]{1,0:T(8,128)(2,1)S(1)}, u32[]{:S(2)}, u32[]{:S(2)}) collective-permute-start(bf16[32,1024]{1,0:T(8,128)(2,1)S(1)} %get-tuple-element.25), channel_id=1, source_target_pairs={{0,4},{4,8},{8,12},{12,16},{16,20},{20,24},{24,28},{28,32},{32,36}... | collective-permute-start | bytes 196616 | tf_op jit(solution)/shard_map/ppermute | solution.py:609
  136.0 1.9 %collective-permute-start.3 = (bf16[32,1024]{1,0:T(8,128)(2,1)S(1)}, bf16[32,1024]{1,0:T(8,128)(2,1)S(1)}, u32[]{:S(2)}, u32[]{:S(2)}) collective-permute-start(bf16[32,1024]{1,0:T(8,128)(2,1)S(1)} %get-tuple-element.26), channel_id=1, source_target_pairs={{0,508},{4,0},{8,4},{12,8},{16,12},{20,16},{24,20},{28,24},{32,28}... | collective-permute-start | bytes 196616 | tf_op jit(solution)/shard_map/ppermute | solution.py:608
  138.0 1.5 %shard_map.129.local_ref = f32[8,256,128]{2,1,0:T(8,128)S(1)} custom-call(bf16[288,128]{1,0:T(8,128)(2,1)S(1)} %reshape.115.refs_1_.kernel_ref, bf16[4,8,32,1024]{3,2,1,0:T(8,128)(2,1)S(1)} %copy-done.3, f32[72,1024]{1,0:T(8,128)S(1)} %fusion.3.plain_ref.mask_ref), custom_call_target="tpu_custom_call" | custom-call | flops 1000000000 | bytes 3514368 | tf_op jit(solution)/shard_map/pallas_call | solution.py:59
  139.5 4.2 %all-to-all-done.5 = bf16[384,2,128]{2,1,0:T(2,128)(2,1)S(1)} async-done(((bf16[384,2,128]{2,1,0:T(2,128)(2,1)}), bf16[384,2,128]{2,1,0:T(2,128)(2,1)S(1)}, u32[]{:S(2)}, u32[]{:S(2)}) %all-to-all-start.5) | async-done | bytes 196640 | tf_op jit(solution)/shard_map/all_to_all | solution.py:463
  (65 shorter events, 11.1 us)
Async XLA Ops:
  7.2 22.4 %copy-start.9 = (bf16[9,32,128]{2,1,0:T(8,128)(2,1)S(1)}, bf16[9,32,128]{2,1,0:T(8,128)(2,1)}, u32[]{:S(2)}) copy-start(bf16[9,32,128]{2,1,0:T(8,128)(2,1)} %param.12) | copy-start | bytes 221188
  7.2 22.8 %copy-start.14 = (s32[8,16]{1,0:T(8,128)S(1)}, s32[8,16]{1,0:T(8,128)}, u32[]{:S(2)}) copy-start(s32[8,16]{1,0:T(8,128)} %param.15) | copy-start | bytes 1540
  7.2 22.8 %copy-start.13 = (s32[8,16,6]{1,0,2:T(8,128)S(1)}, s32[8,16,6]{1,0,2:T(8,128)}, u32[]{:S(2)}) copy-start(s32[8,16,6]{1,0,2:T(8,128)} %param.14) | copy-start | bytes 9220
  7.2 62.7 %all-gather.6.cloned.1.call-start = ((), (), s32[]{:S(2)}) async-start(), calls=%async_computation.7 | async-start | bytes 2621440 | tf_op jit(solution)/shard_map/all_gather | solution.py:489
  7.2 23.1 %copy-start.11 = (bf16[3,16,1024,1]{2,1,3,0:T(8,128)(2,1)S(1)}, bf16[3,16,1024,1]{2,1,3,0:T(8,128)(2,1)}, u32[]{:S(2)}) copy-start(bf16[3,16,1024,1]{2,1,3,0:T(8,128)(2,1)} %constant.24) | copy-start | bytes 294916
  9.6 30.1 %copy-start = (bf16[128,2048]{1,0:T(8,128)(2,1)S(1)}, bf16[128,2048]{1,0:T(8,128)(2,1)}, u32[]{:S(2)}) copy-start(bf16[128,2048]{1,0:T(8,128)(2,1)} %constant.14.clone.table_ref) | copy-start | bytes 1572868
  9.6 30.0 %all-to-all-start = ((bf16[128,2,128]{2,1,0:T(2,128)(2,1)}), bf16[128,2,128]{2,1,0:T(2,128)(2,1)S(1)}, u32[]{:S(2)}, u32[]{:S(2)}) async-start(bf16[128,2,128]{2,1,0:T(2,128)(2,1)} %bitcast.64), calls=%async_computation | async-start | bytes 131072 | tf_op jit(solution)/shard_map/all_to_all | solution.py:463
  28.2 16.6 %copy-start.12 = (bf16[16,1024]{1,0:T(8,128)(2,1)S(1)}, bf16[16,1024]{1,0:T(8,128)(2,1)}, u32[]{:S(2)}) copy-start(bf16[16,1024]{1,0:T(8,128)(2,1)} %constant.15.clone) | copy-start | bytes 98308
  29.8 21.2 %copy-start.2 = (bf16[1,128,32,128]{3,2,1,0:T(8,128)(2,1)S(1)}, bf16[1,128,32,128]{3,2,1,0:T(8,128)(2,1)}, u32[]{:S(2)}) copy-start(bf16[1,128,32,128]{3,2,1,0:T(8,128)(2,1)} %param.13) | copy-start | bytes 3145732
  40.8 10.2 %all-to-all-start.1 = ((bf16[4,112,128]{2,1,0:T(8,128)(2,1)}), bf16[4,112,128]{2,1,0:T(8,128)(2,1)S(1)}, u32[]{:S(2)}, u32[]{:S(2)}) async-start(bf16[4,112,128]{2,1,0:T(8,128)(2,1)} %shard_map.123), calls=%async_computation.1 | async-start | bytes 229376 | tf_op jit(solution)/shard_map/all_to_all | solution.py:467
  44.8 85.7 %all-gather.4.cloned.1.call-start = ((), (), s32[]{:S(2)}) async-start(), calls=%async_computation.6 | async-start | bytes 2621440 | tf_op jit(solution)/shard_map/all_gather | solution.py:568
  51.0 25.5 %copy-start.10 = (bf16[9,32,128]{2,1,0:T(8,128)(2,1)S(1)}, bf16[9,32,128]{2,1,0:T(8,128)(2,1)}, u32[]{:S(2)}) copy-start(bf16[9,32,128]{2,1,0:T(8,128)(2,1)} %param.12) | copy-start | bytes 221188
  69.9 1.6 %copy-start.4 = (bf16[32,32,1024]{2,1,0:T(8,128)(2,1)S(1)}, bf16[32,32,1024]{2,1,0:T(8,128)(2,1)}, u32[]{:S(2)}) copy-start(bf16[32,32,1024]{2,1,0:T(8,128)(2,1)} %all-gather.6.cloned.1.call-done) | copy-start | bytes 6291460
  71.5 5.0 %copy-start.5 = (bf16[32,32,1024]{2,1,0:T(8,128)(2,1)S(1)}, bf16[32,32,1024]{2,1,0:T(8,128)(2,1)}, u32[]{:S(2)}) copy-start(bf16[32,32,1024]{2,1,0:T(8,128)(2,1)} %all-gather.6.cloned.1.call-done) | copy-start | bytes 6291460
  71.5 11.0 %copy-start.6 = (bf16[256,1024]{1,0:T(8,128)(2,1)S(1)}, bf16[256,1024]{1,0:T(8,128)(2,1)}, u32[]{:S(2)}) copy-start(bf16[256,1024]{1,0:T(8,128)(2,1)} %constant.13.clone.table_ref) | copy-start | bytes 1572868
  71.5 6.4 %collective-permute-start = (bf16[4,32,1024]{2,1,0:T(8,128)(2,1)S(1)}, bf16[4,32,1024]{2,1,0:T(8,128)(2,1)S(1)}, u32[]{:S(2)}, u32[]{:S(2)}) collective-permute-start(bf16[4,32,1024]{2,1,0:T(8,128)(2,1)S(1)} %get-tuple-element.18), channel_id=1, source_target_pairs={{0,4},{4,8},{8,12},{12,16},{16,20},{20,24},{24,28},{28,32},{32,36}... | collective-permute-start | bytes 786440 | tf_op jit(solution)/shard_map/ppermute | solution.py:536
  74.6 8.0 %collective-permute-start.1 = (bf16[4,32,1024]{2,1,0:T(8,128)(2,1)S(1)}, bf16[4,32,1024]{2,1,0:T(8,128)(2,1)S(1)}, u32[]{:S(2)}, u32[]{:S(2)}) collective-permute-start(bf16[4,32,1024]{2,1,0:T(8,128)(2,1)S(1)} %get-tuple-element.19), channel_id=1, source_target_pairs={{0,508},{4,0},{8,4},{12,8},{16,12},{20,16},{24,20},{28,24},{32,28}... | collective-permute-start | bytes 786440 | tf_op jit(solution)/shard_map/ppermute | solution.py:537
  87.3 24.5 %all-to-all-start.3 = ((bf16[128,8,128]{2,1,0:T(8,128)(2,1)}), bf16[128,8,128]{2,1,0:T(8,128)(2,1)S(1)}, u32[]{:S(2)}, u32[]{:S(2)}) async-start(bf16[128,8,128]{2,1,0:T(8,128)(2,1)} %bitcast.55), calls=%async_computation.3 | async-start | bytes 524288 | tf_op jit(solution)/shard_map/all_to_all | solution.py:463
  113.7 7.5 %all-to-all-start.4 = ((bf16[4,32,128]{2,1,0:T(8,128)(2,1)}), bf16[4,32,128]{2,1,0:T(8,128)(2,1)S(1)}, u32[]{:S(2)}, u32[]{:S(2)}) async-start(bf16[4,32,128]{2,1,0:T(8,128)(2,1)} %bitcast.17), calls=%async_computation.4 | async-start | bytes 65536 | tf_op jit(solution)/shard_map/all_to_all | solution.py:467
  117.7 14.8 %copy-start.1 = (bf16[1,128,32,128]{3,2,1,0:T(8,128)(2,1)}, bf16[1,128,32,128]{3,2,1,0:T(8,128)(2,1)S(1)}, u32[]{:S(2)}) copy-start(bf16[1,128,32,128]{3,2,1,0:T(8,128)(2,1)S(1)} %multiply_convert_fusion.refs_0_) | copy-start | bytes 3145732
  122.4 21.3 %all-to-all-start.5 = ((bf16[384,2,128]{2,1,0:T(2,128)(2,1)}), bf16[384,2,128]{2,1,0:T(2,128)(2,1)S(1)}, u32[]{:S(2)}, u32[]{:S(2)}) async-start(bf16[384,2,128]{2,1,0:T(2,128)(2,1)} %bitcast.22), calls=%async_computation.5 | async-start | bytes 393216 | tf_op jit(solution)/shard_map/all_to_all | solution.py:463
  130.5 1.6 %copy-start.3 = (bf16[4,8,32,1024]{3,2,1,0:T(8,128)(2,1)S(1)}, bf16[4,8,32,1024]{3,2,1,0:T(8,128)(2,1)}, u32[]{:S(2)}) copy-start(bf16[4,8,32,1024]{3,2,1,0:T(8,128)(2,1)} %all-gather.4.cloned.1.call-done.grad_ref) | copy-start | bytes 6291460
  132.5 11.2 %collective-permute-start.2 = (bf16[32,1024]{1,0:T(8,128)(2,1)S(1)}, bf16[32,1024]{1,0:T(8,128)(2,1)S(1)}, u32[]{:S(2)}, u32[]{:S(2)}) collective-permute-start(bf16[32,1024]{1,0:T(8,128)(2,1)S(1)} %get-tuple-element.25), channel_id=1, source_target_pairs={{0,4},{4,8},{8,12},{12,16},{16,20},{20,24},{24,28},{28,32},{32,36}... | collective-permute-start | bytes 196616 | tf_op jit(solution)/shard_map/ppermute | solution.py:609
  136.0 7.7 %collective-permute-start.3 = (bf16[32,1024]{1,0:T(8,128)(2,1)S(1)}, bf16[32,1024]{1,0:T(8,128)(2,1)S(1)}, u32[]{:S(2)}, u32[]{:S(2)}) collective-permute-start(bf16[32,1024]{1,0:T(8,128)(2,1)S(1)} %get-tuple-element.26), channel_id=1, source_target_pairs={{0,508},{4,0},{8,4},{12,8},{16,12},{20,16},{24,20},{28,24},{32,28}... | collective-permute-start | bytes 196616 | tf_op jit(solution)/shard_map/ppermute | solution.py:608
  (2 other events, 1.5 us)
Sparse Core Ops, SparseCore 0:
  10.7 42.8 all-gather.5
  87.4 31.6 all-gather.3

commit v4 on v3

--- a/solution.py
+++ b/solution.py
@@ -563,6 +563,7 @@
             pltpu.VMEM((OFFSETS * own, channels), F32),
             eight,
         ],
+        limit=57,
         flops=2 * 10**9,
     )
     all_grad = lax.all_gather(grad_pre.reshape(rows, own, NY), "chan")

time: 153 us -> 155 us (1.013)
  Pallas kernels: 15 us -> 18.2 us
    pallas_call x11, Pallas kernels: 15 us -> 18.2 us  [call(): pl.pallas_call(body, out_shape=shapes, in_specs=[pl.BlockSpec(memory_spac...]
    all_to_all x3, waiting for transfers between devices: 25.1 us -> 26.7 us  [exchange(): lax.all_to_all(cube, 'rows', split_axis=0, concat_axis=0, tiled=True)]
    unnamed x30 -> x36, local copies, waits for them, and re-layouts: 4.72 us -> 4.93 us
  transfers between devices with their start and end apart: 11 -> 11, of which waited for: 6 -> 6; matrix products, arithmetic and copies ran while one was open for 4% -> 3% of each run, Pallas kernels for 5% -> 5%
where the time goes in v4:
time: 155 us; the launch traced here: 154 us
  starting transfers between devices  54.8 us (35%)
  waiting for transfers between devices  39.4 us (25%)
  Pallas kernels  18.2 us (12%)
  blocking collectives  18.1 us (12%)
  between operations  14.5 us (9%)
  local copies, waits for them, and re-layouts  8.01 us (5%)
    all_to_all x3, starting transfers between devices, exchange(): lax.all_to_all(cube, 'rows', split_axis=0, concat_axis=0, tiled=True)  36.9 us
    all_to_all x3, waiting for transfers between devices, exchange(): lax.all_to_all(cube, 'rows', split_axis=0, concat_axis=0, tiled=True)  26.7 us
    pallas_call x11, Pallas kernels, call(): pl.pallas_call(body, out_shape=shapes, in_specs=[pl.BlockSpec(memory_spac...  18.2 us
    all_to_all x1, blocking collectives, exchange(): lax.all_to_all(cube, 'rows', split_axis=0, concat_axis=0, tiled=True)  18.1 us
    all_to_all x2, waiting for transfers between devices, swap(): lax.all_to_all(values, 'chan', split_axis=0, concat_axis=0, tiled=True)  9.03 us
    all_to_all x2, starting transfers between devices, swap(): lax.all_to_all(values, 'chan', split_axis=0, concat_axis=0, tiled=True)  7.28 us
    unnamed x36, local copies, waits for them, and re-layouts  4.93 us
    ppermute x1, starting transfers between devices, on_device(): from_low = lax.ppermute(to_high, 'rows', forward)  3.68 us
  transfers between devices with their start and end apart: 11, of which 6 were waited for; matrix products, arithmetic and copies ran while one was open for 3% of the time, Pallas kernels for 5%

profile of v4, /device:TPU:1, one launch (start us, length us, event | category | flops | bytes accessed | tf_op | source)
XLA Modules:
  0.0 154.2 jit_solution(7668399547574610380)
XLA Ops:
  7.3 2.3 %shard_map.121 = (bf16[256,128]{1,0:T(8,128)(2,1)}, bf16[8,32,1024]{2,1,0:T(8,128)(2,1)}) custom-call(bf16[256,1024]{1,0:T(8,128)(2,1)} %bitcast.58, bf16[256,1024]{1,0:T(8,128)(2,1)} %constant.13.clone.table_ref), custom_call_target="tpu_custom_call" | custom-call | flops 100000000 | bytes 589824 | tf_op jit(solution)/shard_map/pallas_call | solution.py:59
  9.6 18.6 %all-to-all-start = ((bf16[128,2,128]{2,1,0:T(2,128)(2,1)}), bf16[128,2,128]{2,1,0:T(2,128)(2,1)S(1)}, u32[]{:S(2)}, u32[]{:S(2)}) async-start(bf16[128,2,128]{2,1,0:T(2,128)(2,1)} %bitcast.64), calls=%async_computation | async-start | bytes 131072 | tf_op jit(solution)/shard_map/all_to_all | solution.py:463
  28.2 1.3 copy.41
  30.5 9.1 %all-to-all-done = bf16[128,2,128]{2,1,0:T(2,128)(2,1)S(1)} async-done(((bf16[128,2,128]{2,1,0:T(2,128)(2,1)}), bf16[128,2,128]{2,1,0:T(2,128)(2,1)S(1)}, u32[]{:S(2)}, u32[]{:S(2)}) %all-to-all-start) | async-done | bytes 65568 | tf_op jit(solution)/shard_map/all_to_all | solution.py:463
  40.8 4.0 %all-to-all-start.1 = ((bf16[4,112,128]{2,1,0:T(8,128)(2,1)}), bf16[4,112,128]{2,1,0:T(8,128)(2,1)S(1)}, u32[]{:S(2)}, u32[]{:S(2)}) async-start(bf16[4,112,128]{2,1,0:T(8,128)(2,1)} %shard_map.123), calls=%async_computation.1 | async-start | bytes 229376 | tf_op jit(solution)/shard_map/all_to_all | solution.py:467
  45.4 5.5 %all-to-all-done.1.got_ref = bf16[4,112,128]{2,1,0:T(8,128)(2,1)S(1)} async-done(((bf16[4,112,128]{2,1,0:T(8,128)(2,1)}), bf16[4,112,128]{2,1,0:T(8,128)(2,1)S(1)}, u32[]{:S(2)}, u32[]{:S(2)}) %all-to-all-start.1) | async-done | bytes 114720 | tf_op jit(solution)/shard_map/all_to_all | solution.py:467
  51.7 18.1 %all_to_all.30 = bf16[128,2,128]{2,1,0:T(2,128)(2,1)S(1)} all-to-all(bf16[128,2,128]{2,1,0:T(2,128)(2,1)S(1)} %bitcast.53), channel_id=1, replica_groups=mesh['rows'=128,'chan'=4] {'rows'}, dimensions={0} | all-to-all | bytes 131072 | tf_op jit(solution)/shard_map/all_to_all | solution.py:463
  69.9 1.6 %copy-done.4 = bf16[32,32,1024]{2,1,0:T(8,128)(2,1)S(1)} copy-done((bf16[32,32,1024]{2,1,0:T(8,128)(2,1)S(1)}, bf16[32,32,1024]{2,1,0:T(8,128)(2,1)}, u32[]{:S(2)}) %copy-start.4) | copy-done | bytes 2097176
  71.6 3.0 %collective-permute-start = (bf16[4,32,1024]{2,1,0:T(8,128)(2,1)S(1)}, bf16[4,32,1024]{2,1,0:T(8,128)(2,1)S(1)}, u32[]{:S(2)}, u32[]{:S(2)}) collective-permute-start(bf16[4,32,1024]{2,1,0:T(8,128)(2,1)S(1)} %get-tuple-element.18), channel_id=1, source_target_pairs={{0,4},{4,8},{8,12},{12,16},{16,20},{20,24},{24,28},{28,32},{32,36}... | collective-permute-start | bytes 786440 | tf_op jit(solution)/shard_map/ppermute | solution.py:536
  74.6 1.9 %collective-permute-start.1 = (bf16[4,32,1024]{2,1,0:T(8,128)(2,1)S(1)}, bf16[4,32,1024]{2,1,0:T(8,128)(2,1)S(1)}, u32[]{:S(2)}, u32[]{:S(2)}) collective-permute-start(bf16[4,32,1024]{2,1,0:T(8,128)(2,1)S(1)} %get-tuple-element.19), channel_id=1, source_target_pairs={{0,508},{4,0},{8,4},{12,8},{16,12},{20,16},{24,20},{28,24},{32,28}... | collective-permute-start | bytes 786440 | tf_op jit(solution)/shard_map/ppermute | solution.py:537
  76.5 1.5 shard_map.122.local_ref
  79.0 3.6 %collective-permute-done.1.high_ref = bf16[4,32,1024]{2,1,0:T(8,128)(2,1)S(1)} collective-permute-done((bf16[4,32,1024]{2,1,0:T(8,128)(2,1)S(1)}, bf16[4,32,1024]{2,1,0:T(8,128)(2,1)S(1)}, u32[]{:S(2)}, u32[]{:S(2)}) %collective-permute-start.1) | collective-permute-done | bytes 262176 | tf_op jit(solution)/shard_map/ppermute | solution.py:537
  83.2 6.3 %shard_map.126 = (bf16[256,1024]{1,0:T(8,128)(2,1)}, bf16[1024,128]{1,0:T(8,128)(2,1)}) custom-call(f32[256,1024]{1,0:T(8,128)} %copy-done.11, bf16[256,128]{1,0:T(8,128)(2,1)} %bitcast.51, bf16[256,1024]{1,0:T(8,128)(2,1)} %bitcast.47, bf16[256,1024]{1,0:T(8,128)(2,1)} %constant.13.clone.table_ref, bf16[4,8,32,1024]{3,2,1,0:T(8,128)(2,1)} %bitcast.43, ...), custom_call_target="tpu_custom_call" | custom-call | flops 2000000000 | bytes 5939200 | tf_op jit(solution)/shard_map/pallas_call | solution.py:59
  89.6 10.3 %all-to-all-start.3 = ((bf16[128,8,128]{2,1,0:T(8,128)(2,1)}), bf16[128,8,128]{2,1,0:T(8,128)(2,1)S(1)}, u32[]{:S(2)}, u32[]{:S(2)}) async-start(bf16[128,8,128]{2,1,0:T(8,128)(2,1)} %bitcast.62), calls=%async_computation.3 | async-start | bytes 524288 | tf_op jit(solution)/shard_map/all_to_all | solution.py:463
  100.6 13.5 %all-to-all-done.3 = bf16[128,8,128]{2,1,0:T(8,128)(2,1)S(1)} async-done(((bf16[128,8,128]{2,1,0:T(8,128)(2,1)}), bf16[128,8,128]{2,1,0:T(8,128)(2,1)S(1)}, u32[]{:S(2)}, u32[]{:S(2)}) %all-to-all-start.3) | async-done | bytes 262176 | tf_op jit(solution)/shard_map/all_to_all | solution.py:463
  114.1 1.8 %shard_map.127 = (bf16[32,128]{1,0:T(8,128)(2,1)S(1)}, bf16[128,128]{1,0:T(8,128)(2,1)}, f32[8,128]{1,0:T(8,128)S(1)}) custom-call(bf16[1024,128]{1,0:T(8,128)(2,1)S(1)} %bitcast.48, bf16[128,2048]{1,0:T(8,128)(2,1)S(1)} %copy-done, bf16[4096,128]{1,0:T(8,128)(2,1)S(1)} %bitcast.42), custom_call_target="tpu_custom_call" | custom-call | flops 100000000 | bytes 1880064 | tf_op jit(solution)/shard_map/pallas_call | solution.py:59
  116.0 3.3 %all-to-all-start.4 = ((bf16[4,32,128]{2,1,0:T(8,128)(2,1)}), bf16[4,32,128]{2,1,0:T(8,128)(2,1)S(1)}, u32[]{:S(2)}, u32[]{:S(2)}) async-start(bf16[4,32,128]{2,1,0:T(8,128)(2,1)} %bitcast.17), calls=%async_computation.4 | async-start | bytes 65536 | tf_op jit(solution)/shard_map/all_to_all | solution.py:467
  120.1 3.5 %all-to-all-done.4.parts_ref = bf16[4,32,128]{2,1,0:T(8,128)(2,1)S(1)} async-done(((bf16[4,32,128]{2,1,0:T(8,128)(2,1)}), bf16[4,32,128]{2,1,0:T(8,128)(2,1)S(1)}, u32[]{:S(2)}, u32[]{:S(2)}) %all-to-all-start.4) | async-done | bytes 32800 | tf_op jit(solution)/shard_map/all_to_all | solution.py:467
  124.7 8.1 %all-to-all-start.5 = ((bf16[384,2,128]{2,1,0:T(2,128)(2,1)}), bf16[384,2,128]{2,1,0:T(2,128)(2,1)S(1)}, u32[]{:S(2)}, u32[]{:S(2)}) async-start(bf16[384,2,128]{2,1,0:T(2,128)(2,1)} %bitcast.22), calls=%async_computation.5 | async-start | bytes 393216 | tf_op jit(solution)/shard_map/all_to_all | solution.py:463
  132.9 1.6 %copy-done.3 = bf16[4,8,32,1024]{3,2,1,0:T(8,128)(2,1)S(1)} copy-done((bf16[4,8,32,1024]{3,2,1,0:T(8,128)(2,1)S(1)}, bf16[4,8,32,1024]{3,2,1,0:T(8,128)(2,1)}, u32[]{:S(2)}) %copy-start.3) | copy-done | bytes 2097176
  134.8 3.7 %collective-permute-start.2 = (bf16[32,1024]{1,0:T(8,128)(2,1)S(1)}, bf16[32,1024]{1,0:T(8,128)(2,1)S(1)}, u32[]{:S(2)}, u32[]{:S(2)}) collective-permute-start(bf16[32,1024]{1,0:T(8,128)(2,1)S(1)} %get-tuple-element.25), channel_id=1, source_target_pairs={{0,4},{4,8},{8,12},{12,16},{16,20},{20,24},{24,28},{28,32},{32,36}... | collective-permute-start | bytes 196616 | tf_op jit(solution)/shard_map/ppermute | solution.py:610
  138.5 1.9 %collective-permute-start.3 = (bf16[32,1024]{1,0:T(8,128)(2,1)S(1)}, bf16[32,1024]{1,0:T(8,128)(2,1)S(1)}, u32[]{:S(2)}, u32[]{:S(2)}) collective-permute-start(bf16[32,1024]{1,0:T(8,128)(2,1)S(1)} %get-tuple-element.26), channel_id=1, source_target_pairs={{0,508},{4,0},{8,4},{12,8},{16,12},{20,16},{24,20},{28,24},{32,28}... | collective-permute-start | bytes 196616 | tf_op jit(solution)/shard_map/ppermute | solution.py:609
  140.5 1.5 %shard_map.129.local_ref = f32[8,256,128]{2,1,0:T(8,128)S(1)} custom-call(bf16[288,128]{1,0:T(8,128)(2,1)S(1)} %reshape.115.refs_1_.kernel_ref, bf16[4,8,32,1024]{3,2,1,0:T(8,128)(2,1)S(1)} %copy-done.3, f32[72,1024]{1,0:T(8,128)S(1)} %fusion.3.plain_ref.mask_ref), custom_call_target="tpu_custom_call" | custom-call | flops 1000000000 | bytes 3514368 | tf_op jit(solution)/shard_map/pallas_call | solution.py:59
  142.0 4.1 %all-to-all-done.5 = bf16[384,2,128]{2,1,0:T(2,128)(2,1)S(1)} async-done(((bf16[384,2,128]{2,1,0:T(2,128)(2,1)}), bf16[384,2,128]{2,1,0:T(2,128)(2,1)S(1)}, u32[]{:S(2)}, u32[]{:S(2)}) %all-to-all-start.5) | async-done | bytes 196640 | tf_op jit(solution)/shard_map/all_to_all | solution.py:463
  (71 shorter events, 9.5 us)
Async XLA Ops:
  7.2 22.4 %copy-start.10 = (bf16[9,32,128]{2,1,0:T(8,128)(2,1)S(1)}, bf16[9,32,128]{2,1,0:T(8,128)(2,1)}, u32[]{:S(2)}) copy-start(bf16[9,32,128]{2,1,0:T(8,128)(2,1)} %param.12) | copy-start | bytes 221188
  7.2 22.8 %copy-start.15 = (s32[8,16]{1,0:T(8,128)S(1)}, s32[8,16]{1,0:T(8,128)}, u32[]{:S(2)}) copy-start(s32[8,16]{1,0:T(8,128)} %param.15) | copy-start | bytes 1540
  7.2 22.8 %copy-start.14 = (s32[8,16,6]{1,0,2:T(8,128)S(1)}, s32[8,16,6]{1,0,2:T(8,128)}, u32[]{:S(2)}) copy-start(s32[8,16,6]{1,0,2:T(8,128)} %param.14) | copy-start | bytes 9220
  7.2 62.7 %all-gather.6.cloned.1.call-start = ((), (), s32[]{:S(2)}) async-start(), calls=%async_computation.7 | async-start | bytes 2621440 | tf_op jit(solution)/shard_map/all_gather | solution.py:489
  7.2 23.1 %copy-start.12 = (bf16[3,16,1024,1]{2,1,3,0:T(8,128)(2,1)S(1)}, bf16[3,16,1024,1]{2,1,3,0:T(8,128)(2,1)}, u32[]{:S(2)}) copy-start(bf16[3,16,1024,1]{2,1,3,0:T(8,128)(2,1)} %constant.24) | copy-start | bytes 294916
  9.6 30.1 %copy-start = (bf16[128,2048]{1,0:T(8,128)(2,1)S(1)}, bf16[128,2048]{1,0:T(8,128)(2,1)}, u32[]{:S(2)}) copy-start(bf16[128,2048]{1,0:T(8,128)(2,1)} %constant.14.clone.table_ref) | copy-start | bytes 1572868
  9.6 30.0 %all-to-all-start = ((bf16[128,2,128]{2,1,0:T(2,128)(2,1)}), bf16[128,2,128]{2,1,0:T(2,128)(2,1)S(1)}, u32[]{:S(2)}, u32[]{:S(2)}) async-start(bf16[128,2,128]{2,1,0:T(2,128)(2,1)} %bitcast.64), calls=%async_computation | async-start | bytes 131072 | tf_op jit(solution)/shard_map/all_to_all | solution.py:463
  28.2 16.6 %copy-start.13 = (bf16[16,1024]{1,0:T(8,128)(2,1)S(1)}, bf16[16,1024]{1,0:T(8,128)(2,1)}, u32[]{:S(2)}) copy-start(bf16[16,1024]{1,0:T(8,128)(2,1)} %constant.15.clone) | copy-start | bytes 98308
  29.6 15.7 %copy-start.6 = (bf16[8,32,1024]{2,1,0:T(8,128)(2,1)}, bf16[8,32,1024]{2,1,0:T(8,128)(2,1)S(1)}, u32[]{:S(2)}) copy-start(bf16[8,32,1024]{2,1,0:T(8,128)(2,1)S(1)} %copy.41) | copy-start | bytes 1572868
  29.8 21.2 %copy-start.2 = (bf16[1,128,32,128]{3,2,1,0:T(8,128)(2,1)S(1)}, bf16[1,128,32,128]{3,2,1,0:T(8,128)(2,1)}, u32[]{:S(2)}) copy-start(bf16[1,128,32,128]{3,2,1,0:T(8,128)(2,1)} %param.13) | copy-start | bytes 3145732
  40.8 10.2 %all-to-all-start.1 = ((bf16[4,112,128]{2,1,0:T(8,128)(2,1)}), bf16[4,112,128]{2,1,0:T(8,128)(2,1)S(1)}, u32[]{:S(2)}, u32[]{:S(2)}) async-start(bf16[4,112,128]{2,1,0:T(8,128)(2,1)} %shard_map.123), calls=%async_computation.1 | async-start | bytes 229376 | tf_op jit(solution)/shard_map/all_to_all | solution.py:467
  44.8 88.1 %all-gather.4.cloned.1.call-start = ((), (), s32[]{:S(2)}) async-start(), calls=%async_computation.6 | async-start | bytes 2621440 | tf_op jit(solution)/shard_map/all_gather | solution.py:569
  45.4 31.1 %copy-start.8 = (f32[72,1024]{1,0:T(8,128)}, f32[72,1024]{1,0:T(8,128)S(1)}, u32[]{:S(2)}) copy-start(f32[72,1024]{1,0:T(8,128)S(1)} %reshape.102.mask_ref.turned_ref) | copy-start | bytes 884740
  69.9 8.1 %copy-start.9 = (bf16[128,2,128]{2,1,0:T(2,128)(2,1)}, bf16[128,2,128]{2,1,0:T(2,128)(2,1)S(1)}, u32[]{:S(2)}) copy-start(bf16[128,2,128]{2,1,0:T(2,128)(2,1)S(1)} %all_to_all.30) | copy-start | bytes 196612
  71.5 5.0 %copy-start.5 = (bf16[32,32,1024]{2,1,0:T(8,128)(2,1)S(1)}, bf16[32,32,1024]{2,1,0:T(8,128)(2,1)}, u32[]{:S(2)}) copy-start(bf16[32,32,1024]{2,1,0:T(8,128)(2,1)} %all-gather.6.cloned.1.call-done) | copy-start | bytes 6291460
  71.6 7.4 %collective-permute-start = (bf16[4,32,1024]{2,1,0:T(8,128)(2,1)S(1)}, bf16[4,32,1024]{2,1,0:T(8,128)(2,1)S(1)}, u32[]{:S(2)}, u32[]{:S(2)}) collective-permute-start(bf16[4,32,1024]{2,1,0:T(8,128)(2,1)S(1)} %get-tuple-element.18), channel_id=1, source_target_pairs={{0,4},{4,8},{8,12},{12,16},{16,20},{20,24},{24,28},{28,32},{32,36}... | collective-permute-start | bytes 786440 | tf_op jit(solution)/shard_map/ppermute | solution.py:536
  74.6 8.0 %collective-permute-start.1 = (bf16[4,32,1024]{2,1,0:T(8,128)(2,1)S(1)}, bf16[4,32,1024]{2,1,0:T(8,128)(2,1)S(1)}, u32[]{:S(2)}, u32[]{:S(2)}) collective-permute-start(bf16[4,32,1024]{2,1,0:T(8,128)(2,1)S(1)} %get-tuple-element.19), channel_id=1, source_target_pairs={{0,508},{4,0},{8,4},{12,8},{16,12},{20,16},{24,20},{28,24},{32,28}... | collective-permute-start | bytes 786440 | tf_op jit(solution)/shard_map/ppermute | solution.py:537
  89.6 24.5 %all-to-all-start.3 = ((bf16[128,8,128]{2,1,0:T(8,128)(2,1)}), bf16[128,8,128]{2,1,0:T(8,128)(2,1)S(1)}, u32[]{:S(2)}, u32[]{:S(2)}) async-start(bf16[128,8,128]{2,1,0:T(8,128)(2,1)} %bitcast.62), calls=%async_computation.3 | async-start | bytes 524288 | tf_op jit(solution)/shard_map/all_to_all | solution.py:463
  116.0 7.5 %all-to-all-start.4 = ((bf16[4,32,128]{2,1,0:T(8,128)(2,1)}), bf16[4,32,128]{2,1,0:T(8,128)(2,1)S(1)}, u32[]{:S(2)}, u32[]{:S(2)}) async-start(bf16[4,32,128]{2,1,0:T(8,128)(2,1)} %bitcast.17), calls=%async_computation.4 | async-start | bytes 65536 | tf_op jit(solution)/shard_map/all_to_all | solution.py:467
  120.0 14.8 %copy-start.1 = (bf16[1,128,32,128]{3,2,1,0:T(8,128)(2,1)}, bf16[1,128,32,128]{3,2,1,0:T(8,128)(2,1)S(1)}, u32[]{:S(2)}) copy-start(bf16[1,128,32,128]{3,2,1,0:T(8,128)(2,1)S(1)} %multiply_convert_fusion.refs_0_) | copy-start | bytes 3145732
  124.7 21.4 %all-to-all-start.5 = ((bf16[384,2,128]{2,1,0:T(2,128)(2,1)}), bf16[384,2,128]{2,1,0:T(2,128)(2,1)S(1)}, u32[]{:S(2)}, u32[]{:S(2)}) async-start(bf16[384,2,128]{2,1,0:T(2,128)(2,1)} %bitcast.22), calls=%async_computation.5 | async-start | bytes 393216 | tf_op jit(solution)/shard_map/all_to_all | solution.py:463
  134.8 11.3 %copy-start.7 = (bf16[256,1024]{1,0:T(8,128)(2,1)S(1)}, bf16[256,1024]{1,0:T(8,128)(2,1)}, u32[]{:S(2)}) copy-start(bf16[256,1024]{1,0:T(8,128)(2,1)} %constant.13.clone.table_ref) | copy-start | bytes 1572868
  134.8 11.3 %collective-permute-start.2 = (bf16[32,1024]{1,0:T(8,128)(2,1)S(1)}, bf16[32,1024]{1,0:T(8,128)(2,1)S(1)}, u32[]{:S(2)}, u32[]{:S(2)}) collective-permute-start(bf16[32,1024]{1,0:T(8,128)(2,1)S(1)} %get-tuple-element.25), channel_id=1, source_target_pairs={{0,4},{4,8},{8,12},{12,16},{16,20},{20,24},{24,28},{28,32},{32,36}... | collective-permute-start | bytes 196616 | tf_op jit(solution)/shard_map/ppermute | solution.py:610
  138.5 7.6 %collective-permute-start.3 = (bf16[32,1024]{1,0:T(8,128)(2,1)S(1)}, bf16[32,1024]{1,0:T(8,128)(2,1)S(1)}, u32[]{:S(2)}, u32[]{:S(2)}) collective-permute-start(bf16[32,1024]{1,0:T(8,128)(2,1)S(1)} %get-tuple-element.26), channel_id=1, source_target_pairs={{0,508},{4,0},{8,4},{12,8},{16,12},{20,16},{24,20},{28,24},{32,28}... | collective-permute-start | bytes 196616 | tf_op jit(solution)/shard_map/ppermute | solution.py:609
  (5 other events, 8.5 us)
Sparse Core Ops, SparseCore 0:
  10.7 42.8 all-gather.5
  89.7 31.6 all-gather.3
